TPU v7x, 512 devices: a whole 4x4x16 slice. The times are simulated.
512 devices in a mesh: region: 8 (over y, core), dom: 64 (over z, x).
Axes of the slice: x: 4, y: 4, z: 16, core: 2. Of those that a mesh axis runs over, the one named last changes fastest.
Arguments:
- flow_state: float32 [13312, 162], P(('region', 'dom')), may hold values from -6 to 6
- right_side: float32 [13312, 162], P(('region', 'dom')), may hold values from -6 to 6
- diag_block: bfloat16 [13312, 26244], P(('region', 'dom')), may hold values from -0.6 to 4.6
- face_scale: bfloat16 [13312, 4, 162], P(('region', 'dom')), may hold values from 0.25 to 2.5
- face_pattern: int32 [13312, 4], P(('region', 'dom')), may hold values from 0 to 5
- neighbour: int32 [13312, 4], P(('region', 'dom')), may hold values from -1 to 77, as said below
- templates: bfloat16 [54, 6, 162], replicated, may hold values from -0.875 to 0.875
- line_inverse: bfloat16 [32768, 26244], P(('region', 'dom')), may hold values from -0.25 to 1.25
- line_scale: bfloat16 [32768, 2, 162], P(('region', 'dom')), may hold values from 0.25 to 2.5
- line_pattern: int32 [32768, 2], P(('region', 'dom')), may hold values from 0 to 5
- elem_line: int32 [13312], P(('region', 'dom')), may hold values from 0 to 4095, as said below
Outputs:
- new_state: float32 [13312, 162], P(('region', 'dom'))
- residual: float32 [13312, 162], P(('region', 'dom'))
Inputs may be any that keep to these rules, and one draw needn't show every extreme that they name: `elem_line`: value owner * 64 + line * 32 + position, owner in 0..63 within the element's region. Within a region every slot holds at most one element, and the filled positions of each line of 32 form a prefix of length 1 or more. The elements of one partition fill at most 1 slots of one line owner, reached in every draw; in every region some line owner has all 64 slots filled. -1 where a side has no neighbour; otherwise a row in three blocks of 26 elements: the partition of the same dom index in the previous region, the own partition, that of the next region. The neighbour meets the element with its opposite side.
All inputs are finite; a program needn't handle non-finite values.
Results may differ from a plain program's by a relative error of at most 0.0033.
Values may be sent and summed in bfloat16 or wider, within the bound.
A program may use at most 64 MiB of HBM per device.

v0:
```python
import jax
import jax.numpy as jnp
from jax import lax
from jax.sharding import PartitionSpec as P

NV = 6
NPAT = 6
LEN = 32
LPD = 2


HIGHEST = lax.Precision.HIGHEST
OPPOSITE = (1, 0, 3, 2)


def extended(cells, sides, width):
    for axis, dim in sides:
        count = lax.axis_size(axis)
        ends = count - 1
        head = lax.slice_in_dim(cells, 0, width, axis=dim)
        tail = lax.slice_in_dim(cells, cells.shape[dim] - width, cells.shape[dim], axis=dim)
        cells = jnp.concatenate(
            [
                lax.ppermute(tail, axis, [(i, (i + 1) % count) for i in range(ends)]),
                cells,
                lax.ppermute(head, axis, [((i + 1) % count, i) for i in range(ends)]),
            ],
            axis=dim,
        )
    return cells


def face_trace(values, face_id):
    nodal = values.reshape(values.shape[:-1] + (NV, 3, 3, 3))
    if face_id == 0:
        picked = nodal[..., 0, :, :]
    elif face_id == 1:
        picked = nodal[..., 2, :, :]
    elif face_id == 2:
        picked = nodal[..., :, 0, :]
    elif face_id == 3:
        picked = nodal[..., :, 2, :]
    elif face_id == 4:
        picked = nodal[..., 0]
    else:
        picked = nodal[..., 2]
    return picked.reshape(values.shape[:-1] + (NV * 9,))


def choose_pattern(all_terms, patterns):
    select = (patterns[:, None] == jnp.arange(NPAT)[None, :]).astype(jnp.float32)
    return jnp.sum(select[:, :, None] * all_terms, axis=1)


def pattern_terms(traces, patterns, face_table):
    all_terms = jnp.dot(traces, face_table, preferred_element_type=jnp.float32)
    return choose_pattern(all_terms.reshape(traces.shape[0], NPAT, -1), patterns)


def exact_terms(traces, patterns, wide_table):
    all_terms = jnp.dot(traces, wide_table, precision=HIGHEST)
    return choose_pattern(all_terms.reshape(traces.shape[0], NPAT, -1), patterns)


def shift_down(values):
    return jnp.concatenate([jnp.zeros_like(values[:, :1]), values[:, :-1]], axis=1)


def shift_up(values):
    return jnp.concatenate([values[:, 1:], jnp.zeros_like(values[:, :1])], axis=1)


def local(
    flow_state,
    right_side,
    diag_block,
    face_scale,
    face_pattern,
    neighbour,
    templates,
    line_inverse,
    line_scale,
    line_pattern,
    elem_line,
):
    elem_count = flow_state.shape[0]
    block_width = flow_state.shape[1]
    trace_width = templates.shape[0]
    slot_total = line_inverse.shape[0]
    owner_index = lax.axis_index("dom")
    face_table = templates.reshape(trace_width, NPAT * block_width)
    rounded = flow_state.astype(jnp.bfloat16)
    widened = extended(rounded, (("region", 0),), elem_count)
    own_blocks = diag_block.reshape(elem_count, block_width, block_width)
    own_term = jnp.einsum("ebc,ec->eb", own_blocks, rounded, preferred_element_type=jnp.float32)
    present = (neighbour >= 0).astype(jnp.float32)
    fetched = jnp.take(
        widened, jnp.clip(neighbour, 0, 3 * elem_count - 1).reshape(-1), axis=0
    ).reshape(elem_count, 4, block_width)
    far_traces = jnp.stack(
        [face_trace(fetched[:, face_index], OPPOSITE[face_index]) for face_index in range(4)],
        axis=1,
    )
    coupled = pattern_terms(
        far_traces.reshape(elem_count * 4, trace_width), face_pattern.reshape(-1), face_table
    )
    coupled = (
        coupled.reshape(elem_count, 4, block_width)
        * face_scale.astype(jnp.float32)
        * present[:, :, None]
    )
    partial_value = right_side - own_term - jnp.sum(coupled, axis=1)
    payload = jnp.stack([rounded.astype(jnp.float32), partial_value], axis=1)
    slot_ids = jnp.arange(slot_total)
    first_slot = (owner_index * slot_total).astype(jnp.float32)
    values = lax.all_gather(payload, "dom", axis=0, tiled=True)
    labels = lax.all_gather(elem_line.astype(jnp.float32), "dom", axis=0, tiled=True)
    select = (labels[None, :] == first_slot + slot_ids[:, None].astype(jnp.float32)).astype(
        jnp.float32
    )
    gathered = jnp.einsum("sr,rcb->scb", select, values, precision=HIGHEST)
    slot_hits = jnp.sum(select, axis=1)
    filled = (slot_hits > 0.5).reshape(LPD, LEN)
    position = jnp.arange(LEN)
    lower_on = (filled & (position[None, :] > 0)).astype(jnp.float32)
    upper_on = shift_up(filled.astype(jnp.float32))
    line_states = gathered[:, 0].astype(jnp.bfloat16)
    top_traces = face_trace(line_states, 5).reshape(LPD, LEN, trace_width)
    bottom_traces = face_trace(line_states, 4).reshape(LPD, LEN, trace_width)
    prev_tops = shift_down(top_traces).reshape(slot_total, trace_width)
    next_bottoms = shift_up(bottom_traces).reshape(slot_total, trace_width)
    scales = line_scale.astype(jnp.float32)
    lower_gate = lower_on.reshape(-1)[:, None]
    upper_gate = upper_on.reshape(-1)[:, None]
    lower_term = (
        pattern_terms(prev_tops, line_pattern[:, 0], face_table) * scales[:, 0] * lower_gate
    )
    upper_term = (
        pattern_terms(next_bottoms, line_pattern[:, 1], face_table) * scales[:, 1] * upper_gate
    )
    line_rhs = gathered[:, 1] - lower_term - upper_term
    lower_scale = scales[:, 0] * lower_gate
    upper_scale = scales[:, 1] * upper_gate
    wide_table = face_table.astype(jnp.float32)
    inverse_lines = line_inverse.reshape(LPD, LEN, block_width, block_width)
    rhs_lines = line_rhs.reshape(LPD, LEN, block_width)
    lower_lines = lower_scale.reshape(LPD, LEN, block_width)
    upper_lines = upper_scale.reshape(LPD, LEN, block_width)
    lower_kind = line_pattern[:, 0].reshape(LPD, LEN)
    upper_kind = line_pattern[:, 1].reshape(LPD, LEN)

    def forward(prev_top, place):
        blocks = lax.dynamic_index_in_dim(inverse_lines, place, 1, keepdims=False).astype(
            jnp.float32
        )
        coupling = lax.dynamic_index_in_dim(lower_lines, place, 1, keepdims=False) * exact_terms(
            prev_top, lax.dynamic_index_in_dim(lower_kind, place, 1, keepdims=False), wide_table
        )
        forced = lax.dynamic_index_in_dim(rhs_lines, place, 1, keepdims=False) - coupling
        solved = jnp.einsum("lbc,lc->lb", blocks, forced, precision=HIGHEST)
        return (face_trace(solved, 5), solved)

    _, sweep_out = lax.scan(forward, jnp.zeros((LPD, trace_width), jnp.float32), position)
    interim = jnp.swapaxes(sweep_out, 0, 1)

    def backward(next_bottom, place):
        blocks = lax.dynamic_index_in_dim(inverse_lines, place, 1, keepdims=False).astype(
            jnp.float32
        )
        coupling = lax.dynamic_index_in_dim(upper_lines, place, 1, keepdims=False) * exact_terms(
            next_bottom, lax.dynamic_index_in_dim(upper_kind, place, 1, keepdims=False), wide_table
        )
        corrected = lax.dynamic_index_in_dim(interim, place, 1, keepdims=False) - jnp.einsum(
            "lbc,lc->lb", blocks, coupling, precision=HIGHEST
        )
        return (face_trace(corrected, 4), corrected)

    _, back_out = lax.scan(
        backward, jnp.zeros((LPD, trace_width), jnp.float32), position, reverse=True
    )
    correction = jnp.swapaxes(back_out, 0, 1).reshape(slot_total, block_width)
    returned_rows = jnp.stack([correction, line_rhs], axis=1)
    portion = lax.all_gather(returned_rows, "dom", axis=0, tiled=True)
    row_index = jnp.arange(portion.shape[0])
    select = (elem_line[:, None] == row_index[None, :]).astype(jnp.float32)
    result = jnp.einsum("er,rcb->ecb", select, portion, precision=HIGHEST)
    return (flow_state + result[:, 0], result[:, 1])


def solution(mesh):
    return jax.shard_map(
        local,
        mesh=mesh,
        in_specs=(
            P(("region", "dom"), None),
            P(("region", "dom"), None),
            P(("region", "dom"), None),
            P(("region", "dom"), None, None),
            P(("region", "dom"), None),
            P(("region", "dom"), None),
            P(),
            P(("region", "dom"), None),
            P(("region", "dom"), None, None),
            P(("region", "dom"), None),
            P(("region", "dom")),
        ),
        out_specs=(P(("region", "dom"), None), P(("region", "dom"), None)),
        check_vma=False,
    )
```

profile of v0, /device:TPU:1, one launch (start us, length us, event | category | flops | bytes accessed | tf_op | source)
XLA Modules:
  0.0 654.0 jit_solution(14775751150099595266)
XLA Ops:
  8.0 8.8 %collective-permute-start.1 = (bf16[26,162]{1,0:T(8,128)(2,1)S(1)}, bf16[26,162]{1,0:T(8,128)(2,1)S(1)}, u32[]{:S(2)}, u32[]{:S(2)}) collective-permute-start(bf16[26,162]{1,0:T(8,128)(2,1)S(1)} %get-tuple-element.327), channel_id=1, source_target_pairs={{64,0},{128,64},{192,128},{256,192},{320,256},{384,320},{448,384},... | collective-permute-start | bytes 25280 | tf_op jit(solution)/shard_map/ppermute | solution.py:26
  16.8 1.9 collective-permute-start
  21.2 4.6 reshape.303
  31.5 1.3 dynamic-slice
  33.6 120.4 %all-reduce.3 = f32[1664]{0:T(1024)S(1)} all-reduce(f32[1664]{0:T(1024)S(1)} %convert_dynamic-update-slice_fusion), channel_id=1, replica_groups=mesh['region'=8,'dom'=64] {'dom'}, use_global_device_ids=true, to_apply=%add.3 | all-reduce | flops 1664 | bytes 13312
  154.7 11.0 %reshape.302 = bf16[2,32,162,162]{3,2,1,0:T(8,128)(2,1)} reshape(bf16[64,26244]{1,0:T(8,128)(2,1)} %param.22) | data formatting | bytes 6718464 | tf_op jit(solution)/shard_map/reshape | solution.py:145
  165.7 2.0 all-gather.3.cloned.1.call-done
  167.7 3.4 fusion.16
  172.7 151.5 %while.28 = (s32[]{:T(128)}, f32[2,54]{1,0:T(2,128)S(1)}, f32[32,2,162]{2,1,0:T(2,128)S(1)}, s32[32]{0:T(128)S(1)}, bf16[2,32,162,162]{3,2,1,0:T(8,128)(2,1)}, /...) while((s32[]{:T(128)}, f32[2,54]{1,0:T(2,128)S(1)}, ...), condition=%wide.region_7.8_spmd, body=%wide.region_5.7_spmd.sunk | while | flops 1893809 | bytes 439091 | solution.py:163
  175.8 1.1 fusion.80
  180.5 1.1 fusion.80
  185.2 1.1 fusion.80
  190.0 1.1 fusion.80
  194.7 1.1 fusion.80
  199.4 1.1 fusion.80
  208.9 1.1 fusion.80
  213.6 1.1 fusion.80
  218.4 1.1 fusion.80
  223.1 1.1 fusion.80
  227.8 1.1 fusion.80
  256.2 1.1 fusion.80
  261.0 1.1 fusion.80
  265.7 1.1 fusion.80
  270.4 1.1 fusion.80
  298.8 1.1 fusion.80
  303.6 1.1 fusion.80
  308.3 1.1 fusion.80
  313.0 1.1 fusion.80
  317.8 1.1 fusion.80
  324.2 148.3 %while.29 = (s32[]{:T(128)}, f32[2,54]{1,0:T(2,128)S(1)}, f32[32,2,162]{2,1,0:T(2,128)S(1)}, s32[32]{0:T(128)S(1)}, f32[2,32,162]{2,0,1:T(2,128)S(1)}, /*index=5...) while((s32[]{:T(128)}, f32[2,54]{1,0:T(2,128)S(1)}, ...), condition=%wide.region_10.11_spmd, body=%wide.region_8.10_spmd.sunk | while | flops 1893810 | bytes 436723 | solution.py:178
  327.3 1.1 fusion.88
  336.6 1.1 fusion.88
  345.8 1.1 fusion.88
  355.1 1.1 fusion.88
  364.4 1.1 fusion.88
  373.6 1.1 fusion.88
  382.9 1.1 fusion.88
  396.8 1.1 fusion.88
  406.1 1.1 fusion.88
  415.3 1.1 fusion.88
  424.6 1.1 fusion.88
  433.9 1.1 fusion.88
  443.1 1.1 fusion.88
  452.4 1.1 fusion.88
  461.7 1.1 fusion.88
  471.0 1.1 fusion.88
  473.2 166.2 %all-gather.5.cloned.1.call-done = f32[4096,2,162]{2,0,1:T(8,128)} async-done(((f32[64,2,162]{2,0,1:T(8,128)}), f32[4096,2,162]{2,0,1:T(8,128)}) %all-gather.5.cloned.1.call-update) | async-done | bytes 5308432 | tf_op jit(solution)/shard_map/all_gather | solution.py:183
  639.5 6.5 fusion.22
  (943 shorter events, 143.7 us)
Async XLA Ops:
  7.2 19.6 %copy-start = (bf16[54,6,162]{2,0,1:T(8,128)(2,1)S(1)}, bf16[54,6,162]{2,0,1:T(8,128)(2,1)}, u32[]{:S(2)}) copy-start(bf16[54,6,162]{2,0,1:T(8,128)(2,1)} %param.21) | copy-start | bytes 314932
  7.2 160.6 %all-gather.3.cloned.1.call-start = ((), (), s32[]{:S(2)}) async-start(), calls=%async_computation | async-start | bytes 3461120 | tf_op jit(solution)/shard_map/all_gather | solution.py:116
  8.0 19.3 %collective-permute-start.1 = (bf16[26,162]{1,0:T(8,128)(2,1)S(1)}, bf16[26,162]{1,0:T(8,128)(2,1)S(1)}, u32[]{:S(2)}, u32[]{:S(2)}) collective-permute-start(bf16[26,162]{1,0:T(8,128)(2,1)S(1)} %get-tuple-element.327), channel_id=1, source_target_pairs={{64,0},{128,64},{192,128},{256,192},{320,256},{384,320},{448,384},... | collective-permute-start | bytes 25280 | tf_op jit(solution)/shard_map/ppermute | solution.py:26
  16.8 10.5 %collective-permute-start = (bf16[26,162]{1,0:T(8,128)(2,1)S(1)}, bf16[26,162]{1,0:T(8,128)(2,1)S(1)}, u32[]{:S(2)}, u32[]{:S(2)}) collective-permute-start(bf16[26,162]{1,0:T(8,128)(2,1)S(1)} %get-tuple-element.327), channel_id=1, source_target_pairs={{0,64},{64,128},{128,192},{192,256},{256,320},{320,384},{384,448},... | collective-permute-start | bytes 25280 | tf_op jit(solution)/shard_map/ppermute | solution.py:24
  25.8 4.4 copy-start.3
  25.8 4.6 copy-start.4
  25.9 5.5 copy-start.5
  25.9 7.6 %copy-start.6 = (s32[26]{0:T(128)S(1)}, s32[26]{0:T(128)}, u32[]{:S(2)}) copy-start(s32[26]{0:T(128)} %param.25) | copy-start | bytes 316
  31.1 608.3 %all-gather.5.cloned.1.call-start = ((), (), s32[]{:S(2)}) async-start(), calls=%async_computation.1 | async-start | bytes 8519680 | tf_op jit(solution)/shard_map/all_gather | solution.py:183
  154.7 11.0 %copy-start.2 = (bf16[64,2,162]{2,1,0:T(2,128)(2,1)S(1)}, bf16[64,2,162]{2,1,0:T(2,128)(2,1)}, u32[]{:S(2)}) copy-start(bf16[64,2,162]{2,1,0:T(2,128)(2,1)} %param.23) | copy-start | bytes 124420
  473.2 173.3 %copy-start.1 = (f32[26,162]{1,0:T(8,128)S(1)}, f32[26,162]{1,0:T(8,128)}, u32[]{:S(2)}) copy-start(f32[26,162]{1,0:T(8,128)} %param.15) | copy-start | bytes 50548
Sparse Core Ops, SparseCore 0:
  31.2 136.4 all-gather.2
  473.4 166.0 all-gather.4
where the time goes:
time: 665 us; the launch traced here: 654 us
  waiting for transfers between devices  168 us (25%)
  loops' own time  128 us (19%)
  blocking collectives  120 us (18%)
  matrix products  98.6 us (15%)
  local copies, waits for them, and re-layouts  97.5 us (15%)
  other arithmetic  15.5 us (2%)
  between operations  15.2 us (2%)
  starting transfers between devices  10.8 us (2%)
    all_gather x1, waiting for transfers between devices, local(): portion = lax.all_gather(returned_rows, 'dom', axis=0, tiled=True)  166 us
    unnamed x1, blocking collectives  120 us
    another operation x1, loops' own time, local(): lax.scan(backward, jnp.zeros((LPD, trace_width), jnp.float32), position,...  63.9 us
    another operation x1, loops' own time, local(): lax.scan(forward, jnp.zeros((LPD, trace_width), jnp.float32), position)  63.8 us
    dynamic_slice x64, local copies, waits for them, and re-layouts, local(): lax.scan(forward, jnp.zeros((LPD, trace_width), jnp.float32), position)  37.5 us
    dot_general x32, matrix products, forward(): solved = jnp.einsum('lbc,lc->lb', blocks, forced, precision=HIGHEST)  36.7 us
    dot_general x32, matrix products, backward(): jnp.einsum('lbc,lc->lb', blocks, coupling, precision=HIGHEST)  36.7 us
    dot_general x64, matrix products, exact_terms(): all_terms = jnp.dot(traces, wide_table, precision=HIGHEST)  14 us
  transfers between devices with their start and end apart: 4, of which 2 were waited for; matrix products, arithmetic and copies ran while one was open for 3% of the time, Pallas kernels for 0%

commit v1 on v0

v1 whole, which is shorter than its diff:
```python
import functools

import jax
import jax.numpy as jnp
import numpy as np
from jax import lax
from jax.experimental import pallas as pl
from jax.experimental.pallas import tpu as pltpu
from jax.sharding import PartitionSpec as P

MESH = pl.DeviceIdType.MESH
F32, BF16 = jnp.float32, jnp.bfloat16
HIGHEST = lax.Precision.HIGHEST
OPPOSITE = (1, 0, 3, 2)

NV = 6
NPAT = 6
LEN = 32
BLOCK = 162
TRACE = 54
ELEM = 26
SLOTS = 64
EROWS = 32
WIDE = 256
TSTEP = 64
TALL = NPAT * TSTEP
MROWS = 56
MSG = 384


def trace_rows(face_id):
    rows = np.arange(BLOCK).reshape(NV, 3, 3, 3)
    a, b, c = (slice(None),) * 3
    if face_id < 2:
        a = 2 * face_id
    elif face_id < 4:
        b = 2 * (face_id - 2)
    else:
        c = 2 * (face_id - 4)
    return rows[:, a, b, c].reshape(-1)


def trace_picks():
    picks = np.zeros((4, WIDE, TALL), np.float32)
    for side in range(4):
        rows = trace_rows(OPPOSITE[side])
        for pattern in range(NPAT):
            picks[side, rows, pattern * TSTEP + np.arange(TRACE)] = 1.0
    return picks


def line_picks():
    picks = np.zeros((WIDE, 128), np.float32)
    picks[trace_rows(5), np.arange(TRACE)] = 1.0
    picks[trace_rows(4), TSTEP + np.arange(TRACE)] = 1.0
    return picks


def dot(a, b, **kw):
    return jnp.dot(a, b, preferred_element_type=F32, **kw)


def lanes(rows, width):
    return lax.broadcasted_iota(jnp.int32, (rows, width), 1)


def halves(x):
    high = x.astype(BF16)
    return high, (x - high.astype(F32)).astype(BF16)


def block_row(ref, rows, start, stop):
    base = pl.multiple_of((start // 128) * 128, 128)
    shift = lax.rem(128 - (start - base), 128)
    tiles = [ref[0:rows, pl.ds(pl.multiple_of(base + 128 * t, 128), 128)].astype(F32) for t in range(3)]
    moved = [pltpu.roll(tile, shift, 1) for tile in tiles]
    keep = lanes(rows, 128) < 128 - (start - base)
    return jnp.concatenate([jnp.where(keep, moved[0], moved[1]), jnp.where(keep, moved[1], moved[2])], axis=1)


def lane_sums(product):
    return jnp.sum(product[:, 0:128] + product[:, 128:256], axis=1, keepdims=True)


def masked_terms(x, patterns, gate, table):
    spread = jnp.concatenate([x, x, x], axis=1)
    rows = x.shape[0]
    spread = jnp.where((lanes(rows, TALL) // TSTEP).astype(F32) == patterns, spread * gate, 0.0)
    return spread


def kernel(
    groups,
    owners,
    fs_ref,
    rs_ref,
    diag_hbm,
    fsc_ref,
    fp_ref,
    nb_ref,
    tmpl_ref,
    linv_hbm,
    lsc_ref,
    lp_ref,
    el_ref,
    picks_ref,
    lpick_ref,
    ns_out,
    res_out,
    diag,
    linv,
    ints,
    xs,
    st,
    tf,
    tp,
    slab,
    mm,
    nn,
    kk,
    own,
    gg,
    hh,
    ff,
    bb,
    cc,
    rhs_s,
    send,
    recv,
    back,
    ret,
    dsem,
    ssem,
    rsem,
):
    reg = lax.axis_index("region")
    me = lax.axis_index("dom")

    bar = pltpu.get_barrier_semaphore()
    below, above = lax.rem(reg + groups - 1, groups), lax.rem(reg + 1, groups)

    def greet(i, carry):
        pl.semaphore_signal(bar, inc=1, device_id=(reg, lax.rem(me + i, owners)), device_id_type=MESH)
        return carry

    pl.semaphore_signal(bar, inc=1, device_id=(below, me), device_id_type=MESH)
    pl.semaphore_signal(bar, inc=1, device_id=(above, me), device_id_type=MESH)
    lax.fori_loop(1, owners, greet, 0)
    get_diag = pltpu.make_async_copy(diag_hbm, diag, dsem.at[0])
    get_linv = pltpu.make_async_copy(linv_hbm, linv, dsem.at[1])
    get_diag.start()
    get_linv.start()

    ints[...] = jnp.full((16, 128), -1.0, F32)
    ints[0:4, 0:ELEM] = nb_ref[...].astype(F32)
    ints[4:8, 0:ELEM] = fp_ref[...].astype(F32)
    ints[8:9, 0:ELEM] = el_ref[...].astype(F32)
    ints[9:11, 0:SLOTS] = lp_ref[...].astype(F32)
    columns = jnp.transpose(ints[...])

    xs[...] = jnp.zeros((EROWS, WIDE), F32)
    xs[0:ELEM, 0:BLOCK] = fs_ref[...]
    rounded = xs[...].astype(BF16)
    st[1] = rounded
    wide_state = rounded.astype(F32)

    tf[...] = jnp.zeros((TALL, WIDE), F32)
    for pattern in range(NPAT):
        tf[pattern * TSTEP : pattern * TSTEP + TRACE, 0:BLOCK] = tmpl_ref[pattern].astype(F32)
    tp[...] = tf[...].astype(BF16)

    get_diag.wait()
    own[...] = jnp.zeros((EROWS, WIDE), F32)
    elem_lane = lanes(ELEM, WIDE)

    def own_rows(b, carry):
        value = lane_sums(block_row(diag, ELEM, b * BLOCK, None) * wide_state[0:ELEM])
        own[0:ELEM] = jnp.where(elem_lane == b, value, own[0:ELEM])
        return carry

    lax.fori_loop(0, BLOCK - 1, own_rows, 0)
    tail = diag[:, (BLOCK - 1) * BLOCK - 98 : BLOCK * BLOCK].astype(F32)
    xs[0:ELEM, 0:BLOCK] = tail[:, 98 : 98 + BLOCK]
    value = lane_sums(xs[...] * wide_state)
    own[...] = jnp.where(lanes(EROWS, WIDE) == BLOCK - 1, value, own[...])

    pl.semaphore_wait(bar, owners + 1)
    up = pltpu.make_async_remote_copy(
        src_ref=st.at[1], dst_ref=st.at[0], send_sem=ssem.at[0], recv_sem=rsem.at[0], device_id=(above, me), device_id_type=MESH
    )
    down = pltpu.make_async_remote_copy(
        src_ref=st.at[1], dst_ref=st.at[2], send_sem=ssem.at[1], recv_sem=rsem.at[1], device_id=(below, me), device_id_type=MESH
    )
    up.start()
    down.start()
    up.wait()
    down.wait()

    stacked = jnp.concatenate([st[0], st[1], st[2]], axis=0)
    row_lane = lanes(EROWS, 3 * EROWS).astype(F32)
    has_below = jnp.where(reg > 0, 1.0, 0.0)
    has_above = jnp.where(reg < groups - 1, 1.0, 0.0)
    pieces = []
    for side in range(4):
        near = columns[0:EROWS, side : side + 1]
        part = jnp.where(near >= ELEM, 1.0, 0.0) + jnp.where(near >= 2 * ELEM, 1.0, 0.0)
        place = near + (EROWS - ELEM) * part
        present = jnp.where(part == 0.0, has_below, jnp.where(part == 2.0, has_above, 1.0))
        pick = jnp.where(row_lane == place, present, 0.0).astype(BF16)
        fetched = dot(pick, stacked).astype(BF16)
        spread = dot(fetched, picks_ref[side])
        pattern = columns[0:EROWS, 4 + side : 5 + side]
        pieces.append(jnp.where((lanes(EROWS, TALL) // TSTEP).astype(F32) == pattern, spread, 0.0).astype(BF16))
    terms = dot(jnp.concatenate(pieces, axis=0), tp[...])
    total = own[...]
    for side in range(4):
        total = total + terms[side * EROWS : (side + 1) * EROWS] * fsc_ref[side]
    xs[...] = jnp.zeros((EROWS, WIDE), F32)
    xs[0:ELEM, 0:BLOCK] = rs_ref[...]
    partial = xs[...] - total

    slot = columns[0:EROWS, 8:9]
    owner = jnp.floor(slot * (1.0 / SLOTS))
    local_slot = slot - owner * SLOTS
    traces = dot(rounded, lpick_ref[...])
    traces = jnp.where(lanes(EROWS, 128) == 127, local_slot + 1.0, traces)
    owner_row = jnp.floor(ints[8:9, 0:EROWS] * (1.0 / SLOTS))
    pick_owner = jnp.where(lax.broadcasted_iota(jnp.int32, (owners, EROWS), 0).astype(F32) == owner_row, 1.0, 0.0)
    payload = jnp.concatenate([traces, partial], axis=1)
    send[:, 0, :] = dot(pick_owner, payload, precision=HIGHEST)

    def exchange(source, target, index):
        def one(i, carry):
            other = lax.rem(me + i, owners)
            pltpu.make_async_remote_copy(
                src_ref=source.at[other],
                dst_ref=target.at[me],
                send_sem=ssem.at[index],
                recv_sem=rsem.at[index],
                device_id=(reg, other),
                device_id_type=MESH,
            ).start()
            return carry

        lax.fori_loop(1, owners, one, 0)
        target[pl.ds(me, 1)] = source[pl.ds(me, 1)]

    def finish(source, target, index):
        whole = pltpu.make_async_remote_copy(
            src_ref=source.at[pl.ds(0, owners - 1)],
            dst_ref=target.at[pl.ds(0, owners - 1)],
            send_sem=ssem.at[index],
            recv_sem=rsem.at[index],
            device_id=(reg, lax.rem(me + 1, owners)),
            device_id_type=MESH,
        )
        whole.wait_send()
        whole.wait_recv()

    exchange(send, recv, 2)

    get_linv.wait()

    def rows_of(b, carry):
        slab[b] = block_row(linv, SLOTS, b * BLOCK, None)
        return carry

    lax.fori_loop(0, BLOCK - 1, rows_of, 0)
    tail = linv[:, (BLOCK - 1) * BLOCK - 98 : BLOCK * BLOCK].astype(F32)
    slab[BLOCK - 1] = jnp.zeros((SLOTS, WIDE), F32)
    slab[BLOCK - 1, :, 0:BLOCK] = tail[:, 98 : 98 + BLOCK]

    kinds = [columns[0:SLOTS, 9 + i : 10 + i] for i in range(2)]
    chosen = [jnp.where((lanes(SLOTS, TALL) // TSTEP).astype(F32) == kind, 1.0, 0.0) for kind in kinds]
    low_half = lanes(SLOTS, 128) < TSTEP

    def small_rows(m, carry):
        first, last = slab[3 * m], slab[3 * m + 2]
        scaled = [last * lsc_ref[0], first * lsc_ref[0], first * lsc_ref[1]]
        parts = [halves(x) for x in scaled]
        stack = jnp.concatenate([p[0] for p in parts] + [p[1] for p in parts], axis=0)
        product = lax.dot_general(stack, tp[...], (((1,), (1,)), ((), ())), preferred_element_type=F32)
        product = product[0 : 3 * SLOTS] + product[3 * SLOTS :]
        for i, (target, kind) in enumerate(((mm, 0), (kk, 0), (nn, 1))):
            x = product[i * SLOTS : (i + 1) * SLOTS] * chosen[kind]
            x = x[:, 0:128] + x[:, 128:256] + x[:, 256:384]
            x = jnp.where(low_half, x + pltpu.roll(x, TSTEP, 1), 0.0)
            if target is kk:
                kk[m] = x
            else:
                target[pl.ds(m, SLOTS, stride=MROWS), :] = x
        return carry

    lax.fori_loop(0, TRACE, small_rows, 0)
    for m in range(TRACE, MROWS):
        mm[pl.ds(m, SLOTS, stride=MROWS), :] = jnp.zeros((SLOTS, 128), F32)
        nn[pl.ds(m, SLOTS, stride=MROWS), :] = jnp.zeros((SLOTS, 128), F32)

    finish(send, recv, 2)
    got = recv[:, 0, :]
    slot_column = got[:, 127:128] - 1.0
    to_slot = jnp.where(lanes(owners, SLOTS).astype(F32) == slot_column, 1.0, 0.0)
    from_source = jnp.transpose(to_slot)
    gathered = dot(from_source, got, precision=HIGHEST)
    filled = jnp.sum(from_source, axis=1, keepdims=True)
    place = lax.rem(lax.broadcasted_iota(jnp.int32, (SLOTS, 1), 0), LEN)
    lower = jnp.where(place > 0, filled, 0.0)
    upper = jnp.where(place < LEN - 1, pltpu.roll(jnp.broadcast_to(filled, (SLOTS, 128)), SLOTS - 1, 0)[:, 0:1], 0.0)

    def coupled(traces_before, traces_after):
        spreads = []
        for x, kind, gate in ((traces_before, 0, lower), (traces_after, 1, upper)):
            x = jnp.where(low_half & (gate > 0.5), x, 0.0)
            x = x + pltpu.roll(x, TSTEP, 1)
            spreads.append(jnp.concatenate([x, x, x], axis=1) * chosen[kind])
        x = jnp.concatenate(spreads, axis=0)
        high, low = halves(x)
        terms = dot(jnp.concatenate([high, low], axis=0), tp[...])
        terms = terms[0 : 2 * SLOTS] + terms[2 * SLOTS :]
        return terms[0:SLOTS] * lsc_ref[0] + terms[SLOTS:] * lsc_ref[1]

    line_traces = gathered[:, 0:128]
    tops = pltpu.roll(line_traces, 1, 0)
    bottoms = pltpu.roll(pltpu.roll(line_traces, TSTEP, 1), SLOTS - 1, 0)
    rhs = gathered[:, 128:384] - coupled(tops, bottoms)
    rhs_s[...] = rhs

    slot_lane = lanes(SLOTS, 128)
    gg[...] = jnp.zeros((SLOTS, 128), F32)
    hh[...] = jnp.zeros((SLOTS, 128), F32)

    def ends(m, carry):
        given = rhs_s[...]
        gg[...] = jnp.where(slot_lane == m, lane_sums(slab[3 * m + 2] * given), gg[...])
        hh[...] = jnp.where(slot_lane == m, lane_sums(slab[3 * m] * given), hh[...])
        return carry

    lax.fori_loop(0, TRACE, ends, 0)

    eye = jnp.where(lanes(MROWS, 128) == lax.broadcasted_iota(jnp.int32, (MROWS, 128), 0), 1.0, 0.0)

    def sweep(matrices, given, out, reverse):
        def step(i, carry):
            position = LEN - 1 - i if reverse else i
            after = []
            for line in range(2):
                j = line * LEN + position
                matrix = matrices[pl.ds(pl.multiple_of(j * MROWS, 8), MROWS), :]
                column = jnp.sum(matrix * carry[line], axis=1, keepdims=True)
                row = given[pl.ds(j, 1), :] - jnp.sum(eye * column, axis=0, keepdims=True)
                out[pl.ds(j, 1), :] = row
                after.append(row)
            return tuple(after)

        zero = jnp.zeros((1, 128), F32)
        lax.fori_loop(0, LEN, step, (zero, zero))

    sweep(mm, gg, ff, False)
    before = jnp.where(lower > 0.5, pltpu.roll(ff[...], 1, 0), 0.0)
    ff[...] = before

    def reduce_first(m, carry):
        hh[...] = jnp.where(slot_lane == m, hh[...] - jnp.sum(kk[m] * ff[...], axis=1, keepdims=True), hh[...])
        return carry

    lax.fori_loop(0, TRACE, reduce_first, 0)
    hh[...] = jnp.where(filled > 0.5, hh[...], 0.0)
    sweep(nn, hh, bb, True)
    after = jnp.where(upper > 0.5, pltpu.roll(bb[...], SLOTS - 1, 0), 0.0)
    cc[...] = rhs_s[...] - coupled(before, after)

    send_lane = lanes(SLOTS, WIDE)
    ret[...] = jnp.zeros((SLOTS, WIDE), F32)

    def solve(b, carry):
        ret[...] = jnp.where(send_lane == b, lane_sums(slab[b] * cc[...]), ret[...])
        return carry

    lax.fori_loop(0, BLOCK, solve, 0)
    both = jnp.concatenate([ret[...], rhs_s[...]], axis=1)
    answer = dot(to_slot, both, precision=HIGHEST)
    send[:, 0, :] = jnp.concatenate([answer[:, 0:128], answer[:, 256:384], jnp.where(slot_lane < TSTEP, answer[:, 128:256], pltpu.roll(answer[:, 384:512], TSTEP, 1))], axis=1)
    exchange(send, back, 3)
    finish(send, back, 3)
    answer = dot(jnp.transpose(pick_owner), back[:, 0, :], precision=HIGHEST)
    third = answer[:, 256:384]
    fixed = jnp.concatenate([answer[:, 0:128], third], axis=1)
    kept = jnp.concatenate([answer[:, 128:256], pltpu.roll(third, TSTEP, 1)], axis=1)
    ns_out[...] = fs_ref[...] + fixed[0:ELEM, 0:BLOCK]
    res_out[...] = kept[0:ELEM, 0:BLOCK]


def local(groups, owners, flow_state, right_side, diag_block, face_scale, face_pattern, neighbour, templates, line_inverse, line_scale, line_pattern, elem_line):
    face_scales = jnp.pad(jnp.transpose(face_scale, (1, 0, 2)).astype(F32), ((0, 0), (0, EROWS - ELEM), (0, WIDE - BLOCK)))
    line_scales = jnp.pad(jnp.transpose(line_scale, (1, 0, 2)).astype(F32), ((0, 0), (0, 0), (0, WIDE - BLOCK)))
    operands = (
        flow_state,
        right_side,
        diag_block,
        face_scales,
        face_pattern.T,
        neighbour.T,
        jnp.transpose(templates, (1, 0, 2)),
        line_inverse,
        line_scales,
        line_pattern.T,
        elem_line[None, :],
        jnp.asarray(trace_picks(), BF16),
        jnp.asarray(line_picks(), BF16),
    )
    vmem = pl.BlockSpec(memory_space=pltpu.VMEM)
    anywhere = pl.BlockSpec(memory_space=pl.ANY)
    message = pltpu.VMEM((owners, 1, MSG), F32)
    return pl.pallas_call(
        functools.partial(kernel, groups, owners),
        out_shape=(jax.ShapeDtypeStruct((ELEM, BLOCK), F32), jax.ShapeDtypeStruct((ELEM, BLOCK), F32)),
        in_specs=[vmem, vmem, anywhere, vmem, vmem, vmem, vmem, anywhere, vmem, vmem, vmem, vmem, vmem],
        out_specs=(vmem, vmem),
        scratch_shapes=[
            pltpu.VMEM((ELEM, BLOCK * BLOCK), BF16),
            pltpu.VMEM((SLOTS, BLOCK * BLOCK), BF16),
            pltpu.VMEM((16, 128), F32),
            pltpu.VMEM((EROWS, WIDE), F32),
            pltpu.VMEM((3, EROWS, WIDE), BF16),
            pltpu.VMEM((TALL, WIDE), F32),
            pltpu.VMEM((TALL, WIDE), BF16),
            pltpu.VMEM((BLOCK, SLOTS, WIDE), F32),
            pltpu.VMEM((SLOTS * MROWS, 128), F32),
            pltpu.VMEM((SLOTS * MROWS, 128), F32),
            pltpu.VMEM((TRACE, SLOTS, 128), F32),
            pltpu.VMEM((EROWS, WIDE), F32),
            pltpu.VMEM((SLOTS, 128), F32),
            pltpu.VMEM((SLOTS, 128), F32),
            pltpu.VMEM((SLOTS, 128), F32),
            pltpu.VMEM((SLOTS, 128), F32),
            pltpu.VMEM((SLOTS, WIDE), F32),
            pltpu.VMEM((SLOTS, WIDE), F32),
            message,
            message,
            message,
            pltpu.VMEM((SLOTS, WIDE), F32),
            pltpu.SemaphoreType.DMA((2,)),
            pltpu.SemaphoreType.DMA((4,)),
            pltpu.SemaphoreType.DMA((4,)),
        ],
        compiler_params=pltpu.CompilerParams(collective_id=0, has_side_effects=True, vmem_limit_bytes=56 * 1024 * 1024),
    )(*operands)


def solution(mesh):
    both = ("region", "dom")
    return jax.shard_map(
        functools.partial(local, mesh.shape["region"], mesh.shape["dom"]),
        mesh=mesh,
        in_specs=(
            P(both, None),
            P(both, None),
            P(both, None),
            P(both, None, None),
            P(both, None),
            P(both, None),
            P(),
            P(both, None),
            P(both, None, None),
            P(both, None),
            P(both),
        ),
        out_specs=(P(both, None), P(both, None)),
        check_vma=False,
    )
```

time: 665 us -> 131 us (0.20); the launches traced: 654 us -> 131 us
  waiting for transfers between devices: 168 us -> 0 us
  loops' own time: 128 us -> 0 us
  Pallas kernels: 0 us -> 124 us
  blocking collectives: 120 us -> 0 us
  matrix products: 98.6 us -> 0 us
  local copies, waits for them, and re-layouts: 97.5 us -> 4.42 us
  between operations: 15.2 us -> 0.65 us
  other arithmetic: 15.5 us -> 1.32 us
  starting transfers between devices: 10.8 us -> 0 us
    all_gather x2 -> x0, waiting for transfers between devices: 168 us -> none  [the longest x1 166 us: local(): portion = lax.all_gather(returned_rows, 'dom', axis=0, tiled=True)]
    another operation x2 -> x0, loops' own time: 128 us -> none  [the longest x1 63.9 us: local(): lax.scan(backward, jnp.zeros((LPD, trace_width), jnp.float32), position,...]
    pallas_call x0 -> x1, Pallas kernels: none -> 124 us  [local(): pl.pallas_call(functools.partial(kernel, groups, owners), out_shape=(jax....]
    unnamed x1 -> x0, blocking collectives: 120 us -> none
    dot_general x134 -> x0, matrix products: 98.6 us -> none  [the longest x32 36.7 us: forward(): solved = jnp.einsum('lbc,lc->lb', blocks, forced, precision=HIGHEST)]
    dynamic_slice x192 -> x0, local copies, waits for them, and re-layouts: 38.7 us -> none  [the longest x64 37.5 us: local(): lax.scan(forward, jnp.zeros((LPD, trace_width), jnp.float32), position)]
    reshape x133 -> x0, local copies, waits for them, and re-layouts: 32.9 us -> none  [the longest x64 11.4 us: face_trace(): nodal = values.reshape(values.shape[:-1] + (NV, 3, 3, 3))]
    slice x79 -> x0, local copies, waits for them, and re-layouts: 12.2 us -> none  [the longest x33 7.25 us: face_trace(): picked = nodal[..., 2]]
  transfers between devices with their start and end apart: 4 -> 0, of which waited for: 2 -> 0; matrix products, arithmetic and copies ran while one was open for 3% -> 0% of each run, Pallas kernels for 0% -> 0%
where the time goes in v1:
time: 131 us
  Pallas kernels  124 us (95%)
  local copies, waits for them, and re-layouts  4.42 us (3%)
  other arithmetic  1.32 us (1%)
    pallas_call x1, Pallas kernels, local(): pl.pallas_call(functools.partial(kernel, groups, owners), out_shape=(jax....  124 us
    unnamed x4, local copies, waits for them, and re-layouts  4.42 us

profile of v1, /device:TPU:1, one launch (start us, length us, event | category | flops | bytes accessed | tf_op | source)
XLA Modules:
  0.0 130.6 jit_solution(15895586485184429611)
XLA Ops:
  0.6 0.8 copy.20
  1.5 0.7 pad_convert_fusion.1.fsc_ref
  2.1 0.8 copy.19
  3.0 0.7 pad_convert_fusion.lsc_ref
  3.6 124.3 %shard_map.140 = (f32[26,162]{1,0:T(8,128)}, f32[26,162]{1,0:T(8,128)}) custom-call(f32[26,162]{1,0:T(8,128)} %fs_ref.1, f32[26,162]{1,0:T(8,128)} %rs_ref.1, bf16[26,26244]{1,0:T(8,128)(2,1)} %diag_hbm.1, f32[4,32,256]{2,1,0:T(8,128)} %pad_convert_fusion.1.fsc_ref, s32[4,26]{1,0:T(4,128)} %bitcast.14, s32[4,26]{1,0:T(4,128)} %bitcast.15, ...), custom_call_target="tpu_custom_call" | custom-call | tf_op jit(solution)/shard_map/pallas_call | solution.py:414
  127.9 1.4 %copy.23 = f32[26,162]{1,0:T(8,128)} copy(f32[26,162]{1,0:T(8,128)} %get-tuple-element.4) | data formatting | bytes 33696
  129.3 1.4 %copy.24 = f32[26,162]{1,0:T(8,128)} copy(f32[26,162]{1,0:T(8,128)} %get-tuple-element.5) | data formatting | bytes 33696

commit v2 on v1

--- a/solution.py
+++ b/solution.py
@@ -28,32 +28,22 @@
 MSG = 384
 
 
-def trace_rows(face_id):
-    rows = np.arange(BLOCK).reshape(NV, 3, 3, 3)
-    a, b, c = (slice(None),) * 3
+def trace_column(face_id, width):
+    k = lax.rem(lanes(1, width), TSTEP).astype(F32)
+    variable, rest = jnp.floor((k + 0.5) * (1.0 / 9.0)), 0.0
+    line = jnp.floor((k + 0.5) * (1.0 / 3.0))
     if face_id < 2:
-        a = 2 * face_id
+        rest = k + 18.0 * variable + 18.0 * face_id
     elif face_id < 4:
-        b = 2 * (face_id - 2)
+        rest = k + 6.0 * line + 6.0 * (face_id - 2)
     else:
-        c = 2 * (face_id - 4)
-    return rows[:, a, b, c].reshape(-1)
-
-
-def trace_picks():
-    picks = np.zeros((4, WIDE, TALL), np.float32)
-    for side in range(4):
-        rows = trace_rows(OPPOSITE[side])
-        for pattern in range(NPAT):
-            picks[side, rows, pattern * TSTEP + np.arange(TRACE)] = 1.0
-    return picks
-
-
-def line_picks():
-    picks = np.zeros((WIDE, 128), np.float32)
-    picks[trace_rows(5), np.arange(TRACE)] = 1.0
-    picks[trace_rows(4), TSTEP + np.arange(TRACE)] = 1.0
-    return picks
+        rest = 3.0 * k + 2.0 * (face_id - 4)
+    return jnp.where(k < TRACE, rest, -1.0)
+
+
+def picks_of(column):
+    rows = lax.broadcasted_iota(jnp.int32, (WIDE, column.shape[1]), 0).astype(F32)
+    return jnp.where(rows == column, 1.0, 0.0).astype(BF16)
 
 
 def dot(a, b, **kw):
@@ -69,7 +59,7 @@
     return high, (x - high.astype(F32)).astype(BF16)
 
 
-def block_row(ref, rows, start, stop):
+def block_row(ref, rows, start):
     base = pl.multiple_of((start // 128) * 128, 128)
     shift = lax.rem(128 - (start - base), 128)
     tiles = [ref[0:rows, pl.ds(pl.multiple_of(base + 128 * t, 128), 128)].astype(F32) for t in range(3)]
@@ -92,21 +82,28 @@
 def kernel(
     groups,
     owners,
+    fs_hbm,
+    rs_hbm,
+    diag_hbm,
+    fsc_hbm,
+    fp_hbm,
+    nb_hbm,
+    tmpl_hbm,
+    linv_hbm,
+    lsc_hbm,
+    lp_hbm,
+    el_hbm,
+    ns_out,
+    res_out,
     fs_ref,
     rs_ref,
-    diag_hbm,
     fsc_ref,
     fp_ref,
     nb_ref,
     tmpl_ref,
-    linv_hbm,
     lsc_ref,
     lp_ref,
     el_ref,
-    picks_ref,
-    lpick_ref,
-    ns_out,
-    res_out,
     diag,
     linv,
     ints,
@@ -114,6 +111,11 @@
     st,
     tf,
     tp,
+    tpt,
+    fsc,
+    lsc,
+    picks,
+    lpick,
     slab,
     mm,
     nn,
@@ -139,17 +141,32 @@
     bar = pltpu.get_barrier_semaphore()
     below, above = lax.rem(reg + groups - 1, groups), lax.rem(reg + 1, groups)
 
+    def others(i):
+        far = owners // 8
+        dz = jnp.where(lax.rem(i, 2) == 1, far - (i + 1) // 2, far + i // 2)
+        z = lax.rem(me // 4 + dz, owners // 4)
+        return [z * 4 + lax.rem(me + dx, 4) for dx in (2, 1, 3, 0)]
+
     def greet(i, carry):
-        pl.semaphore_signal(bar, inc=1, device_id=(reg, lax.rem(me + i, owners)), device_id_type=MESH)
+        for other in others(i):
+            pl.semaphore_signal(bar, inc=1, device_id=(reg, other), device_id_type=MESH)
         return carry
 
     pl.semaphore_signal(bar, inc=1, device_id=(below, me), device_id_type=MESH)
     pl.semaphore_signal(bar, inc=1, device_id=(above, me), device_id_type=MESH)
-    lax.fori_loop(1, owners, greet, 0)
+    lax.fori_loop(0, owners // 4 - 1, greet, 0)
+    for other in others(owners // 4 - 1)[:3]:
+        pl.semaphore_signal(bar, inc=1, device_id=(reg, other), device_id_type=MESH)
     get_diag = pltpu.make_async_copy(diag_hbm, diag, dsem.at[0])
     get_linv = pltpu.make_async_copy(linv_hbm, linv, dsem.at[1])
+    small = ((fs_hbm, fs_ref), (tmpl_hbm, tmpl_ref), (nb_hbm, nb_ref), (fp_hbm, fp_ref), (el_hbm, el_ref), (lp_hbm, lp_ref), (fsc_hbm, fsc_ref), (lsc_hbm, lsc_ref), (rs_hbm, rs_ref))
+    fetches = [pltpu.make_async_copy(source, target, dsem.at[2 + i]) for i, (source, target) in enumerate(small)]
+    for fetch in fetches:
+        fetch.start()
     get_diag.start()
     get_linv.start()
+    for fetch in fetches:
+        fetch.wait()
 
     ints[...] = jnp.full((16, 128), -1.0, F32)
     ints[0:4, 0:ELEM] = nb_ref[...].astype(F32)
@@ -168,21 +185,50 @@
     for pattern in range(NPAT):
         tf[pattern * TSTEP : pattern * TSTEP + TRACE, 0:BLOCK] = tmpl_ref[pattern].astype(F32)
     tp[...] = tf[...].astype(BF16)
+    tpt[...] = jnp.transpose(tf[...]).astype(BF16)
+    fsc[...] = jnp.zeros((4, EROWS, WIDE), F32)
+    for side in range(4):
+        fsc[side, 0:ELEM, 0:BLOCK] = fsc_ref[:, side, :].astype(F32)
+    lsc[...] = jnp.zeros((2, SLOTS, WIDE), F32)
+    for side in range(2):
+        lsc[side, :, 0:BLOCK] = lsc_ref[:, side, :].astype(F32)
+
+    for side in range(4):
+        picks[side] = picks_of(trace_column(OPPOSITE[side], TALL))
+    lpick[...] = picks_of(jnp.where(lanes(1, 128) < TSTEP, trace_column(5, 128), trace_column(4, 128)))
 
     get_diag.wait()
+
+    def own_rows_of(i, carry):
+        for b in range(7):
+            slab[i * 7 + b, 0:ELEM] = block_row(diag, ELEM, (i * 7 + b) * BLOCK)
+        return carry
+
+    lax.fori_loop(0, (BLOCK - 1) // 7, own_rows_of, 0)
+    tail = diag[:, (BLOCK - 1) * BLOCK - 98 : BLOCK * BLOCK].astype(F32)
+    slab[BLOCK - 1, 0:EROWS] = jnp.zeros((EROWS, WIDE), F32)
+    slab[BLOCK - 1, 0:ELEM, 0:BLOCK] = tail[:, 98 : 98 + BLOCK]
     own[...] = jnp.zeros((EROWS, WIDE), F32)
-    elem_lane = lanes(ELEM, WIDE)
-
-    def own_rows(b, carry):
-        value = lane_sums(block_row(diag, ELEM, b * BLOCK, None) * wide_state[0:ELEM])
-        own[0:ELEM] = jnp.where(elem_lane == b, value, own[0:ELEM])
-        return carry
-
-    lax.fori_loop(0, BLOCK - 1, own_rows, 0)
-    tail = diag[:, (BLOCK - 1) * BLOCK - 98 : BLOCK * BLOCK].astype(F32)
-    xs[0:ELEM, 0:BLOCK] = tail[:, 98 : 98 + BLOCK]
-    value = lane_sums(xs[...] * wide_state)
-    own[...] = jnp.where(lanes(EROWS, WIDE) == BLOCK - 1, value, own[...])
+    elem_lane = lanes(EROWS, WIDE)
+
+    def own_rows(i, carry):
+        total = own[...]
+        for b in range(18):
+            b = i * 18 + b
+            total = jnp.where(elem_lane == b, lane_sums(slab[b, 0:EROWS] * wide_state), total)
+        own[...] = total
+        return carry
+
+    lax.fori_loop(0, BLOCK // 18, own_rows, 0)
+
+    get_linv.wait()
+
+    def rows_of(i, carry):
+        for b in range(7):
+            slab[i * 7 + b] = block_row(linv, SLOTS, (i * 7 + b) * BLOCK)
+        return carry
+
+    lax.fori_loop(0, 12, rows_of, 0)
 
     pl.semaphore_wait(bar, owners + 1)
     up = pltpu.make_async_remote_copy(
@@ -193,6 +239,10 @@
     )
     up.start()
     down.start()
+    lax.fori_loop(12, (BLOCK - 1) // 7, rows_of, 0)
+    tail = linv[:, (BLOCK - 1) * BLOCK - 98 : BLOCK * BLOCK].astype(F32)
+    slab[BLOCK - 1] = jnp.zeros((SLOTS, WIDE), F32)
+    slab[BLOCK - 1, :, 0:BLOCK] = tail[:, 98 : 98 + BLOCK]
     up.wait()
     down.wait()
 
@@ -208,13 +258,13 @@
         present = jnp.where(part == 0.0, has_below, jnp.where(part == 2.0, has_above, 1.0))
         pick = jnp.where(row_lane == place, present, 0.0).astype(BF16)
         fetched = dot(pick, stacked).astype(BF16)
-        spread = dot(fetched, picks_ref[side])
+        spread = dot(fetched, picks[side])
         pattern = columns[0:EROWS, 4 + side : 5 + side]
         pieces.append(jnp.where((lanes(EROWS, TALL) // TSTEP).astype(F32) == pattern, spread, 0.0).astype(BF16))
     terms = dot(jnp.concatenate(pieces, axis=0), tp[...])
     total = own[...]
     for side in range(4):
-        total = total + terms[side * EROWS : (side + 1) * EROWS] * fsc_ref[side]
+        total = total + terms[side * EROWS : (side + 1) * EROWS] * fsc[side]
     xs[...] = jnp.zeros((EROWS, WIDE), F32)
     xs[0:ELEM, 0:BLOCK] = rs_ref[...]
     partial = xs[...] - total
@@ -222,7 +272,7 @@
     slot = columns[0:EROWS, 8:9]
     owner = jnp.floor(slot * (1.0 / SLOTS))
     local_slot = slot - owner * SLOTS
-    traces = dot(rounded, lpick_ref[...])
+    traces = dot(rounded, lpick[...])
     traces = jnp.where(lanes(EROWS, 128) == 127, local_slot + 1.0, traces)
     owner_row = jnp.floor(ints[8:9, 0:EROWS] * (1.0 / SLOTS))
     pick_owner = jnp.where(lax.broadcasted_iota(jnp.int32, (owners, EROWS), 0).astype(F32) == owner_row, 1.0, 0.0)
@@ -230,8 +280,7 @@
     send[:, 0, :] = dot(pick_owner, payload, precision=HIGHEST)
 
     def exchange(source, target, index):
-        def one(i, carry):
-            other = lax.rem(me + i, owners)
+        def one(other):
             pltpu.make_async_remote_copy(
                 src_ref=source.at[other],
                 dst_ref=target.at[me],
@@ -240,9 +289,15 @@
                 device_id=(reg, other),
                 device_id_type=MESH,
             ).start()
+
+        def four(i, carry):
+            for other in others(i):
+                one(other)
             return carry
 
-        lax.fori_loop(1, owners, one, 0)
+        lax.fori_loop(0, owners // 4 - 1, four, 0)
+        for other in others(owners // 4 - 1)[:3]:
+            one(other)
         target[pl.ds(me, 1)] = source[pl.ds(me, 1)]
 
     def finish(source, target, index):
@@ -259,39 +314,31 @@
 
     exchange(send, recv, 2)
 
-    get_linv.wait()
-
-    def rows_of(b, carry):
-        slab[b] = block_row(linv, SLOTS, b * BLOCK, None)
-        return carry
-
-    lax.fori_loop(0, BLOCK - 1, rows_of, 0)
-    tail = linv[:, (BLOCK - 1) * BLOCK - 98 : BLOCK * BLOCK].astype(F32)
-    slab[BLOCK - 1] = jnp.zeros((SLOTS, WIDE), F32)
-    slab[BLOCK - 1, :, 0:BLOCK] = tail[:, 98 : 98 + BLOCK]
-
     kinds = [columns[0:SLOTS, 9 + i : 10 + i] for i in range(2)]
     chosen = [jnp.where((lanes(SLOTS, TALL) // TSTEP).astype(F32) == kind, 1.0, 0.0) for kind in kinds]
     low_half = lanes(SLOTS, 128) < TSTEP
 
-    def small_rows(m, carry):
-        first, last = slab[3 * m], slab[3 * m + 2]
-        scaled = [last * lsc_ref[0], first * lsc_ref[0], first * lsc_ref[1]]
-        parts = [halves(x) for x in scaled]
-        stack = jnp.concatenate([p[0] for p in parts] + [p[1] for p in parts], axis=0)
-        product = lax.dot_general(stack, tp[...], (((1,), (1,)), ((), ())), preferred_element_type=F32)
-        product = product[0 : 3 * SLOTS] + product[3 * SLOTS :]
-        for i, (target, kind) in enumerate(((mm, 0), (kk, 0), (nn, 1))):
-            x = product[i * SLOTS : (i + 1) * SLOTS] * chosen[kind]
-            x = x[:, 0:128] + x[:, 128:256] + x[:, 256:384]
-            x = jnp.where(low_half, x + pltpu.roll(x, TSTEP, 1), 0.0)
-            if target is kk:
-                kk[m] = x
-            else:
-                target[pl.ds(m, SLOTS, stride=MROWS), :] = x
-        return carry
-
-    lax.fori_loop(0, TRACE, small_rows, 0)
+    def small_rows(i, carry):
+        parts = []
+        for u in range(3):
+            first, last = slab[3 * (3 * i + u)], slab[3 * (3 * i + u) + 2]
+            for x in (last * lsc[0], first * lsc[0], first * lsc[1]):
+                parts.extend(halves(x))
+        product = dot(jnp.concatenate(parts, axis=0), tpt[...])
+        for u in range(3):
+            m = 3 * i + u
+            for n, (target, kind) in enumerate(((mm, 0), (kk, 0), (nn, 1))):
+                at = (u * 6 + n * 2) * SLOTS
+                x = (product[at : at + SLOTS] + product[at + SLOTS : at + 2 * SLOTS]) * chosen[kind]
+                x = x[:, 0:128] + x[:, 128:256] + x[:, 256:384]
+                x = jnp.where(low_half, x + pltpu.roll(x, TSTEP, 1), 0.0)
+                if target is kk:
+                    kk[m] = x
+                else:
+                    target[pl.ds(m, SLOTS, stride=MROWS), :] = x
+        return carry
+
+    lax.fori_loop(0, TRACE // 3, small_rows, 0)
     for m in range(TRACE, MROWS):
         mm[pl.ds(m, SLOTS, stride=MROWS), :] = jnp.zeros((SLOTS, 128), F32)
         nn[pl.ds(m, SLOTS, stride=MROWS), :] = jnp.zeros((SLOTS, 128), F32)
@@ -317,7 +364,7 @@
         high, low = halves(x)
         terms = dot(jnp.concatenate([high, low], axis=0), tp[...])
         terms = terms[0 : 2 * SLOTS] + terms[2 * SLOTS :]
-        return terms[0:SLOTS] * lsc_ref[0] + terms[SLOTS:] * lsc_ref[1]
+        return terms[0:SLOTS] * lsc[0] + terms[SLOTS:] * lsc[1]
 
     line_traces = gathered[:, 0:128]
     tops = pltpu.roll(line_traces, 1, 0)
@@ -329,13 +376,17 @@
     gg[...] = jnp.zeros((SLOTS, 128), F32)
     hh[...] = jnp.zeros((SLOTS, 128), F32)
 
-    def ends(m, carry):
-        given = rhs_s[...]
-        gg[...] = jnp.where(slot_lane == m, lane_sums(slab[3 * m + 2] * given), gg[...])
-        hh[...] = jnp.where(slot_lane == m, lane_sums(slab[3 * m] * given), hh[...])
-        return carry
-
-    lax.fori_loop(0, TRACE, ends, 0)
+    def ends(i, carry):
+        given, top, bottom = rhs_s[...], gg[...], hh[...]
+        for m in range(9):
+            m = i * 9 + m
+            top = jnp.where(slot_lane == m, lane_sums(slab[3 * m + 2] * given), top)
+            bottom = jnp.where(slot_lane == m, lane_sums(slab[3 * m] * given), bottom)
+        gg[...] = top
+        hh[...] = bottom
+        return carry
+
+    lax.fori_loop(0, TRACE // 9, ends, 0)
 
     eye = jnp.where(lanes(MROWS, 128) == lax.broadcasted_iota(jnp.int32, (MROWS, 128), 0), 1.0, 0.0)
 
@@ -359,11 +410,15 @@
     before = jnp.where(lower > 0.5, pltpu.roll(ff[...], 1, 0), 0.0)
     ff[...] = before
 
-    def reduce_first(m, carry):
-        hh[...] = jnp.where(slot_lane == m, hh[...] - jnp.sum(kk[m] * ff[...], axis=1, keepdims=True), hh[...])
-        return carry
-
-    lax.fori_loop(0, TRACE, reduce_first, 0)
+    def reduce_first(i, carry):
+        total, f = hh[...], ff[...]
+        for m in range(18):
+            m = i * 18 + m
+            total = jnp.where(slot_lane == m, total - jnp.sum(kk[m] * f, axis=1, keepdims=True), total)
+        hh[...] = total
+        return carry
+
+    lax.fori_loop(0, TRACE // 18, reduce_first, 0)
     hh[...] = jnp.where(filled > 0.5, hh[...], 0.0)
     sweep(nn, hh, bb, True)
     after = jnp.where(upper > 0.5, pltpu.roll(bb[...], SLOTS - 1, 0), 0.0)
@@ -372,11 +427,15 @@
     send_lane = lanes(SLOTS, WIDE)
     ret[...] = jnp.zeros((SLOTS, WIDE), F32)
 
-    def solve(b, carry):
-        ret[...] = jnp.where(send_lane == b, lane_sums(slab[b] * cc[...]), ret[...])
-        return carry
-
-    lax.fori_loop(0, BLOCK, solve, 0)
+    def solve(i, carry):
+        total, given = ret[...], cc[...]
+        for b in range(18):
+            b = i * 18 + b
+            total = jnp.where(send_lane == b, lane_sums(slab[b] * given), total)
+        ret[...] = total
+        return carry
+
+    lax.fori_loop(0, BLOCK // 18, solve, 0)
     both = jnp.concatenate([ret[...], rhs_s[...]], axis=1)
     answer = dot(to_slot, both, precision=HIGHEST)
     send[:, 0, :] = jnp.concatenate([answer[:, 0:128], answer[:, 256:384], jnp.where(slot_lane < TSTEP, answer[:, 128:256], pltpu.roll(answer[:, 384:512], TSTEP, 1))], axis=1)
@@ -386,37 +445,42 @@
     third = answer[:, 256:384]
     fixed = jnp.concatenate([answer[:, 0:128], third], axis=1)
     kept = jnp.concatenate([answer[:, 128:256], pltpu.roll(third, TSTEP, 1)], axis=1)
-    ns_out[...] = fs_ref[...] + fixed[0:ELEM, 0:BLOCK]
-    res_out[...] = kept[0:ELEM, 0:BLOCK]
+    ns_out[...] = fixed[0:ELEM, 0:BLOCK]
+    res_out[...] = rs_ref[...] - kept[0:ELEM, 0:BLOCK]
 
 
 def local(groups, owners, flow_state, right_side, diag_block, face_scale, face_pattern, neighbour, templates, line_inverse, line_scale, line_pattern, elem_line):
-    face_scales = jnp.pad(jnp.transpose(face_scale, (1, 0, 2)).astype(F32), ((0, 0), (0, EROWS - ELEM), (0, WIDE - BLOCK)))
-    line_scales = jnp.pad(jnp.transpose(line_scale, (1, 0, 2)).astype(F32), ((0, 0), (0, 0), (0, WIDE - BLOCK)))
     operands = (
         flow_state,
         right_side,
         diag_block,
-        face_scales,
+        face_scale,
         face_pattern.T,
         neighbour.T,
         jnp.transpose(templates, (1, 0, 2)),
         line_inverse,
-        line_scales,
+        line_scale,
         line_pattern.T,
         elem_line[None, :],
-        jnp.asarray(trace_picks(), BF16),
-        jnp.asarray(line_picks(), BF16),
     )
     vmem = pl.BlockSpec(memory_space=pltpu.VMEM)
     anywhere = pl.BlockSpec(memory_space=pl.ANY)
     message = pltpu.VMEM((owners, 1, MSG), F32)
-    return pl.pallas_call(
+    correction, removed = pl.pallas_call(
         functools.partial(kernel, groups, owners),
         out_shape=(jax.ShapeDtypeStruct((ELEM, BLOCK), F32), jax.ShapeDtypeStruct((ELEM, BLOCK), F32)),
-        in_specs=[vmem, vmem, anywhere, vmem, vmem, vmem, vmem, anywhere, vmem, vmem, vmem, vmem, vmem],
+        in_specs=[anywhere] * 11,
         out_specs=(vmem, vmem),
         scratch_shapes=[
+            pltpu.VMEM((ELEM, BLOCK), F32),
+            pltpu.VMEM((ELEM, BLOCK), F32),
+            pltpu.VMEM((ELEM, 4, BLOCK), BF16),
+            pltpu.VMEM((4, ELEM), jnp.int32),
+            pltpu.VMEM((4, ELEM), jnp.int32),
+            pltpu.VMEM((NPAT, TRACE, BLOCK), BF16),
+            pltpu.VMEM((SLOTS, 2, BLOCK), BF16),
+            pltpu.VMEM((2, SLOTS), jnp.int32),
+            pltpu.VMEM((1, ELEM), jnp.int32),
             pltpu.VMEM((ELEM, BLOCK * BLOCK), BF16),
             pltpu.VMEM((SLOTS, BLOCK * BLOCK), BF16),
             pltpu.VMEM((16, 128), F32),
@@ -424,6 +488,11 @@
             pltpu.VMEM((3, EROWS, WIDE), BF16),
             pltpu.VMEM((TALL, WIDE), F32),
             pltpu.VMEM((TALL, WIDE), BF16),
+            pltpu.VMEM((WIDE, TALL), BF16),
+            pltpu.VMEM((4, EROWS, WIDE), F32),
+            pltpu.VMEM((2, SLOTS, WIDE), F32),
+            pltpu.VMEM((4, WIDE, TALL), BF16),
+            pltpu.VMEM((WIDE, 128), BF16),
             pltpu.VMEM((BLOCK, SLOTS, WIDE), F32),
             pltpu.VMEM((SLOTS * MROWS, 128), F32),
             pltpu.VMEM((SLOTS * MROWS, 128), F32),
@@ -439,12 +508,13 @@
             message,
             message,
             pltpu.VMEM((SLOTS, WIDE), F32),
-            pltpu.SemaphoreType.DMA((2,)),
+            pltpu.SemaphoreType.DMA((2 + 9,)),
             pltpu.SemaphoreType.DMA((4,)),
             pltpu.SemaphoreType.DMA((4,)),
         ],
         compiler_params=pltpu.CompilerParams(collective_id=0, has_side_effects=True, vmem_limit_bytes=56 * 1024 * 1024),
     )(*operands)
+    return flow_state + correction, right_side - removed
 
 
 def solution(mesh):

time: 131 us -> 60.7 us (0.46)
  Pallas kernels: 124 us -> 56.9 us
  local copies, waits for them, and re-layouts: 4.42 us -> 0.01 us
  other arithmetic: 1.32 us -> 2.76 us
    pallas_call x1, Pallas kernels: 124 us -> 56.9 us  [local(): pl.pallas_call(functools.partial(kernel, groups, owners), out_shape=(jax....]
    unnamed x4, local copies, waits for them, and re-layouts: 4.42 us -> 0.01 us
    add x0 -> x1, other arithmetic: none -> 1.38 us  [local(): return (flow_state + correction, right_side - removed)]
    sub x0 -> x1, other arithmetic: none -> 1.38 us  [local(): return (flow_state + correction, right_side - removed)]
    pad x2 -> x0, other arithmetic: 1.32 us -> none  [the longest x1 0.66 us: local(): jnp.pad(jnp.transpose(face_scale, (1, 0, 2)).astype(F32), ((0, 0), (0, ER...]
where the time goes in v2:
time: 60.7 us; the launch traced here: 60.4 us
  Pallas kernels  56.9 us (94%)
  other arithmetic  2.76 us (5%)
  between operations  0.67 us (1%)
    pallas_call x1, Pallas kernels, local(): pl.pallas_call(functools.partial(kernel, groups, owners), out_shape=(jax....  56.9 us
    add x1, other arithmetic, local(): return (flow_state + correction, right_side - removed)  1.38 us
    sub x1, other arithmetic, local(): return (flow_state + correction, right_side - removed)  1.38 us

profile of v2, /device:TPU:1, one launch (start us, length us, event | category | flops | bytes accessed | tf_op | source)
XLA Modules:
  0.0 60.4 jit_solution(2806588799499220349)
XLA Ops:
  0.6 0.0 copy-start.1
  0.6 0.0 copy-start
  0.7 56.9 %shard_map.122 = (f32[26,162]{1,0:T(8,128)}, f32[26,162]{1,0:T(8,128)}) custom-call(f32[26,162]{1,0:T(8,128)} %fs_hbm.1, f32[26,162]{1,0:T(8,128)} %rs_hbm.1, bf16[26,26244]{1,0:T(8,128)(2,1)} %diag_hbm.1, bf16[26,4,162]{2,1,0:T(4,128)(2,1)} %fsc_hbm.1, s32[4,26]{1,0:T(4,128)} %bitcast.6, s32[4,26]{1,0:T(4,128)} %bitcast.7, bf16[6,54,162]{2,1,0:T(8,128)(2,1)} %bitcast.5, ...), custom_call_target="tpu_custom_call" | custom-call | tf_op jit(solution)/shard_map/pallas_call | solution.py:469
  57.6 0.0 copy-done
  57.6 1.4 %add.3 = f32[26,162]{1,0:T(8,128)} add(f32[26,162]{1,0:T(8,128)S(1)} %copy-done, f32[26,162]{1,0:T(8,128)} %get-tuple-element.4) | non-fusion elementwise | flops 4212 | bytes 50544 | tf_op jit(solution)/shard_map/add | solution.py:517
  59.0 0.0 copy-done.1
  59.0 1.4 %sub.3 = f32[26,162]{1,0:T(8,128)} subtract(f32[26,162]{1,0:T(8,128)S(1)} %copy-done.1, f32[26,162]{1,0:T(8,128)} %get-tuple-element.5) | non-fusion elementwise | flops 4212 | bytes 50544 | tf_op jit(solution)/shard_map/sub | solution.py:517
Async XLA Ops:
  0.6 58.4 %copy-start.1 = (f32[26,162]{1,0:T(8,128)S(1)}, f32[26,162]{1,0:T(8,128)}, u32[]{:S(2)}) copy-start(f32[26,162]{1,0:T(8,128)} %rs_hbm.1) | copy-start | bytes 50548
  0.6 57.0 %copy-start = (f32[26,162]{1,0:T(8,128)S(1)}, f32[26,162]{1,0:T(8,128)}, u32[]{:S(2)}) copy-start(f32[26,162]{1,0:T(8,128)} %fs_hbm.1) | copy-start | bytes 50548

commit v3 on v2

--- a/solution.py
+++ b/solution.py
@@ -10,7 +10,6 @@
 
 MESH = pl.DeviceIdType.MESH
 F32, BF16 = jnp.float32, jnp.bfloat16
-HIGHEST = lax.Precision.HIGHEST
 OPPOSITE = (1, 0, 3, 2)
 
 NV = 6
@@ -46,12 +45,17 @@
     return jnp.where(rows == column, 1.0, 0.0).astype(BF16)
 
 
-def dot(a, b, **kw):
-    return jnp.dot(a, b, preferred_element_type=F32, **kw)
+def dot(a, b):
+    return jnp.dot(a, b, preferred_element_type=F32)
 
 
 def lanes(rows, width):
     return lax.broadcasted_iota(jnp.int32, (rows, width), 1)
+
+
+def pick_rows(pick, x):
+    pick = pick.astype(BF16)
+    return dot(jnp.concatenate([pick, pick], axis=1), jnp.concatenate(halves(x), axis=0))
 
 
 def halves(x):
@@ -70,13 +74,6 @@
 
 def lane_sums(product):
     return jnp.sum(product[:, 0:128] + product[:, 128:256], axis=1, keepdims=True)
-
-
-def masked_terms(x, patterns, gate, table):
-    spread = jnp.concatenate([x, x, x], axis=1)
-    rows = x.shape[0]
-    spread = jnp.where((lanes(rows, TALL) // TSTEP).astype(F32) == patterns, spread * gate, 0.0)
-    return spread
 
 
 def kernel(
@@ -93,8 +90,7 @@
     lsc_hbm,
     lp_hbm,
     el_hbm,
-    ns_out,
-    res_out,
+    out,
     fs_ref,
     rs_ref,
     fsc_ref,
@@ -111,6 +107,7 @@
     st,
     tf,
     tp,
+    tp2,
     tpt,
     fsc,
     lsc,
@@ -119,12 +116,11 @@
     slab,
     mm,
     nn,
-    kk,
     own,
-    gg,
-    hh,
-    ff,
-    bb,
+    gcol,
+    rows_p,
+    gate_p,
+    out_p,
     cc,
     rhs_s,
     send,
@@ -185,7 +181,11 @@
     for pattern in range(NPAT):
         tf[pattern * TSTEP : pattern * TSTEP + TRACE, 0:BLOCK] = tmpl_ref[pattern].astype(F32)
     tp[...] = tf[...].astype(BF16)
-    tpt[...] = jnp.transpose(tf[...]).astype(BF16)
+    turned = jnp.transpose(tf[...]).astype(BF16)
+    tp2[0:TALL] = tp[...]
+    tp2[TALL:] = tp[...]
+    tpt[0:WIDE] = turned
+    tpt[WIDE:] = turned
     fsc[...] = jnp.zeros((4, EROWS, WIDE), F32)
     for side in range(4):
         fsc[side, 0:ELEM, 0:BLOCK] = fsc_ref[:, side, :].astype(F32)
@@ -200,11 +200,11 @@
     get_diag.wait()
 
     def own_rows_of(i, carry):
-        for b in range(7):
-            slab[i * 7 + b, 0:ELEM] = block_row(diag, ELEM, (i * 7 + b) * BLOCK)
-        return carry
-
-    lax.fori_loop(0, (BLOCK - 1) // 7, own_rows_of, 0)
+        for b in range(23):
+            slab[i * 23 + b, 0:ELEM] = block_row(diag, ELEM, (i * 23 + b) * BLOCK)
+        return carry
+
+    lax.fori_loop(0, (BLOCK - 1) // 23, own_rows_of, 0)
     tail = diag[:, (BLOCK - 1) * BLOCK - 98 : BLOCK * BLOCK].astype(F32)
     slab[BLOCK - 1, 0:EROWS] = jnp.zeros((EROWS, WIDE), F32)
     slab[BLOCK - 1, 0:ELEM, 0:BLOCK] = tail[:, 98 : 98 + BLOCK]
@@ -213,22 +213,22 @@
 
     def own_rows(i, carry):
         total = own[...]
-        for b in range(18):
-            b = i * 18 + b
+        for b in range(54):
+            b = i * 54 + b
             total = jnp.where(elem_lane == b, lane_sums(slab[b, 0:EROWS] * wide_state), total)
         own[...] = total
         return carry
 
-    lax.fori_loop(0, BLOCK // 18, own_rows, 0)
+    lax.fori_loop(0, BLOCK // 54, own_rows, 0)
 
     get_linv.wait()
 
     def rows_of(i, carry):
-        for b in range(7):
-            slab[i * 7 + b] = block_row(linv, SLOTS, (i * 7 + b) * BLOCK)
-        return carry
-
-    lax.fori_loop(0, 12, rows_of, 0)
+        for b in range(23):
+            slab[i * 23 + b] = block_row(linv, SLOTS, (i * 23 + b) * BLOCK)
+        return carry
+
+    lax.fori_loop(0, 4, rows_of, 0)
 
     pl.semaphore_wait(bar, owners + 1)
     up = pltpu.make_async_remote_copy(
@@ -239,7 +239,7 @@
     )
     up.start()
     down.start()
-    lax.fori_loop(12, (BLOCK - 1) // 7, rows_of, 0)
+    lax.fori_loop(4, (BLOCK - 1) // 23, rows_of, 0)
     tail = linv[:, (BLOCK - 1) * BLOCK - 98 : BLOCK * BLOCK].astype(F32)
     slab[BLOCK - 1] = jnp.zeros((SLOTS, WIDE), F32)
     slab[BLOCK - 1, :, 0:BLOCK] = tail[:, 98 : 98 + BLOCK]
@@ -277,7 +277,7 @@
     owner_row = jnp.floor(ints[8:9, 0:EROWS] * (1.0 / SLOTS))
     pick_owner = jnp.where(lax.broadcasted_iota(jnp.int32, (owners, EROWS), 0).astype(F32) == owner_row, 1.0, 0.0)
     payload = jnp.concatenate([traces, partial], axis=1)
-    send[:, 0, :] = dot(pick_owner, payload, precision=HIGHEST)
+    send[:, 0, :] = pick_rows(pick_owner, payload)
 
     def exchange(source, target, index):
         def one(other):
@@ -317,136 +317,144 @@
     kinds = [columns[0:SLOTS, 9 + i : 10 + i] for i in range(2)]
     chosen = [jnp.where((lanes(SLOTS, TALL) // TSTEP).astype(F32) == kind, 1.0, 0.0) for kind in kinds]
     low_half = lanes(SLOTS, 128) < TSTEP
+    own_half = lanes(SLOTS, 128) // TSTEP == lax.broadcasted_iota(jnp.int32, (SLOTS, 128), 0) // LEN
+
+    def store_rows(target, m, x):
+        target[pl.ds(m, LEN, stride=2 * TSTEP), :] = x[0:LEN]
+        target[pl.ds(m + TSTEP, LEN, stride=2 * TSTEP), :] = x[LEN:]
 
     def small_rows(i, carry):
         parts = []
-        for u in range(3):
-            first, last = slab[3 * (3 * i + u)], slab[3 * (3 * i + u) + 2]
-            for x in (last * lsc[0], first * lsc[0], first * lsc[1]):
-                parts.extend(halves(x))
+        for u in range(9):
+            m = 9 * i + u
+            for x in (slab[3 * m + 2] * lsc[0], slab[3 * m] * lsc[1]):
+                parts.append(jnp.concatenate(halves(x), axis=1))
         product = dot(jnp.concatenate(parts, axis=0), tpt[...])
-        for u in range(3):
-            m = 3 * i + u
-            for n, (target, kind) in enumerate(((mm, 0), (kk, 0), (nn, 1))):
-                at = (u * 6 + n * 2) * SLOTS
-                x = (product[at : at + SLOTS] + product[at + SLOTS : at + 2 * SLOTS]) * chosen[kind]
+        for u in range(9):
+            for kind, target in enumerate((mm, nn)):
+                at = (u * 2 + kind) * SLOTS
+                x = product[at : at + SLOTS] * chosen[kind]
                 x = x[:, 0:128] + x[:, 128:256] + x[:, 256:384]
-                x = jnp.where(low_half, x + pltpu.roll(x, TSTEP, 1), 0.0)
-                if target is kk:
-                    kk[m] = x
-                else:
-                    target[pl.ds(m, SLOTS, stride=MROWS), :] = x
-        return carry
-
-    lax.fori_loop(0, TRACE // 3, small_rows, 0)
-    for m in range(TRACE, MROWS):
-        mm[pl.ds(m, SLOTS, stride=MROWS), :] = jnp.zeros((SLOTS, 128), F32)
-        nn[pl.ds(m, SLOTS, stride=MROWS), :] = jnp.zeros((SLOTS, 128), F32)
+                x = x + pltpu.roll(x, TSTEP, 1)
+                store_rows(target, 9 * i + u, jnp.where(own_half, x, 0.0))
+        return carry
+
+    lax.fori_loop(0, TRACE // 9, small_rows, 0)
+    for m in range(TRACE, TSTEP):
+        for target in (mm, nn, gcol):
+            store_rows(target, m, jnp.zeros((SLOTS, 128), F32))
+
+    def turn(i, carry):
+        for target, position in ((mm, 2 * i + 1), (nn, 2 * i)):
+            at = pl.multiple_of(position * 2 * TSTEP, 128)
+            block = target[pl.ds(at, TSTEP), :] + target[pl.ds(at + TSTEP, TSTEP), :]
+            block = jnp.transpose(block)
+            target[pl.ds(at, TSTEP), :] = jnp.concatenate([block[0:TSTEP], block[TSTEP:]], axis=1)
+        return carry
+
+    lax.fori_loop(0, LEN // 2, turn, 0, unroll=8)
 
     finish(send, recv, 2)
     got = recv[:, 0, :]
     slot_column = got[:, 127:128] - 1.0
     to_slot = jnp.where(lanes(owners, SLOTS).astype(F32) == slot_column, 1.0, 0.0)
     from_source = jnp.transpose(to_slot)
-    gathered = dot(from_source, got, precision=HIGHEST)
+    gathered = pick_rows(from_source, got)
     filled = jnp.sum(from_source, axis=1, keepdims=True)
     place = lax.rem(lax.broadcasted_iota(jnp.int32, (SLOTS, 1), 0), LEN)
     lower = jnp.where(place > 0, filled, 0.0)
     upper = jnp.where(place < LEN - 1, pltpu.roll(jnp.broadcast_to(filled, (SLOTS, 128)), SLOTS - 1, 0)[:, 0:1], 0.0)
 
-    def coupled(traces_before, traces_after):
-        spreads = []
-        for x, kind, gate in ((traces_before, 0, lower), (traces_after, 1, upper)):
-            x = jnp.where(low_half & (gate > 0.5), x, 0.0)
-            x = x + pltpu.roll(x, TSTEP, 1)
-            spreads.append(jnp.concatenate([x, x, x], axis=1) * chosen[kind])
-        x = jnp.concatenate(spreads, axis=0)
-        high, low = halves(x)
-        terms = dot(jnp.concatenate([high, low], axis=0), tp[...])
-        terms = terms[0 : 2 * SLOTS] + terms[2 * SLOTS :]
-        return terms[0:SLOTS] * lsc[0] + terms[SLOTS:] * lsc[1]
+    def coupled(kind, gate, x):
+        x = jnp.where(gate > 0.5, x, 0.0)
+        spread = jnp.concatenate([x, x, x], axis=1) * chosen[kind]
+        return dot(jnp.concatenate(halves(spread), axis=1), tp2[...]) * lsc[kind]
 
     line_traces = gathered[:, 0:128]
-    tops = pltpu.roll(line_traces, 1, 0)
-    bottoms = pltpu.roll(pltpu.roll(line_traces, TSTEP, 1), SLOTS - 1, 0)
-    rhs = gathered[:, 128:384] - coupled(tops, bottoms)
+    swapped = pltpu.roll(line_traces, TSTEP, 1)
+    tops = jnp.where(low_half, line_traces, swapped)
+    bottoms = jnp.where(low_half, swapped, line_traces)
+    rhs = gathered[:, 128:384] - coupled(0, lower, pltpu.roll(tops, 1, 0)) - coupled(1, upper, pltpu.roll(bottoms, SLOTS - 1, 0))
     rhs_s[...] = rhs
 
     slot_lane = lanes(SLOTS, 128)
-    gg[...] = jnp.zeros((SLOTS, 128), F32)
-    hh[...] = jnp.zeros((SLOTS, 128), F32)
-
-    def ends(i, carry):
-        given, top, bottom = rhs_s[...], gg[...], hh[...]
-        for m in range(9):
-            m = i * 9 + m
-            top = jnp.where(slot_lane == m, lane_sums(slab[3 * m + 2] * given), top)
-            bottom = jnp.where(slot_lane == m, lane_sums(slab[3 * m] * given), bottom)
-        gg[...] = top
-        hh[...] = bottom
-        return carry
-
-    lax.fori_loop(0, TRACE // 9, ends, 0)
-
-    eye = jnp.where(lanes(MROWS, 128) == lax.broadcasted_iota(jnp.int32, (MROWS, 128), 0), 1.0, 0.0)
-
-    def sweep(matrices, given, out, reverse):
-        def step(i, carry):
-            position = LEN - 1 - i if reverse else i
-            after = []
+    row_lane = lanes(LEN, 128)
+
+    def trace_of_solution(given, first, gate):
+        x, rows = given[...], jnp.zeros((LEN, 128), F32)
+        for m in range(TRACE):
+            value = jnp.broadcast_to(lane_sums(slab[3 * m + first] * x), (SLOTS, 128))
+            if gate is not None:
+                value = jnp.where(gate > 0.5, value, 0.0)
+            store_rows(gcol, m, value)
+            rows = jnp.where(row_lane == m, value[0:LEN], jnp.where(row_lane == m + TSTEP, value[LEN:], rows))
+        rows_p[...] = jnp.broadcast_to(rows[:, None, :], (LEN, 8, 128))
+
+    gates = jnp.where(row_lane < TSTEP, filled[0:LEN], filled[LEN:])
+    gate_p[...] = jnp.broadcast_to(gates[:, None, :], (LEN, 8, 128))
+    trace_of_solution(rhs_s, 2, None)
+
+    tiles = MROWS // 8
+    place8 = [lax.broadcasted_iota(jnp.int32, (tiles, 8, 128), i) for i in range(3)]
+    eye = jnp.where(place8[2] % TSTEP == 8 * place8[0] + place8[1], 1.0, 0.0)
+    first_line = place8[2] < TSTEP
+
+    def sweep(matrices, reverse):
+        def pair(i, row):
+            first = LEN - 1 - 2 * i if reverse else 2 * i
+            second = first - 1 if reverse else first + 1
+            at = pl.multiple_of(first * 2 * TSTEP, 128)
+            column = []
             for line in range(2):
-                j = line * LEN + position
-                matrix = matrices[pl.ds(pl.multiple_of(j * MROWS, 8), MROWS), :]
-                column = jnp.sum(matrix * carry[line], axis=1, keepdims=True)
-                row = given[pl.ds(j, 1), :] - jnp.sum(eye * column, axis=0, keepdims=True)
-                out[pl.ds(j, 1), :] = row
-                after.append(row)
-            return tuple(after)
-
-        zero = jnp.zeros((1, 128), F32)
-        lax.fori_loop(0, LEN, step, (zero, zero))
-
-    sweep(mm, gg, ff, False)
-    before = jnp.where(lower > 0.5, pltpu.roll(ff[...], 1, 0), 0.0)
-    ff[...] = before
-
-    def reduce_first(i, carry):
-        total, f = hh[...], ff[...]
-        for m in range(18):
-            m = i * 18 + m
-            total = jnp.where(slot_lane == m, total - jnp.sum(kk[m] * f, axis=1, keepdims=True), total)
-        hh[...] = total
-        return carry
-
-    lax.fori_loop(0, TRACE // 18, reduce_first, 0)
-    hh[...] = jnp.where(filled > 0.5, hh[...], 0.0)
-    sweep(nn, hh, bb, True)
-    after = jnp.where(upper > 0.5, pltpu.roll(bb[...], SLOTS - 1, 0), 0.0)
-    cc[...] = rhs_s[...] - coupled(before, after)
+                block = pl.ds(at + line * TSTEP, MROWS)
+                product = matrices[block, :].reshape(tiles, 8, 128) * row[None]
+                column.append(gcol[block, :].reshape(tiles, 8, 128) - jnp.sum(product, axis=2, keepdims=True))
+            column = jnp.where(first_line, column[0], column[1])
+            out_p[pl.ds(first, 1), :] = jnp.sum(jnp.sum(eye * column, axis=0), axis=0, keepdims=True)
+            turned = matrices[pl.ds(pl.multiple_of(second * 2 * TSTEP, 128), MROWS), :].reshape(tiles, 8, 128)
+            moved = jnp.sum(jnp.sum(turned * column, axis=0), axis=0, keepdims=True)
+            row = jnp.where(gate_p[second] > 0.5, rows_p[second] - moved, 0.0)
+            out_p[pl.ds(second, 1), :] = row[0:1]
+            return row
+
+        lax.fori_loop(0, LEN // 2, pair, jnp.zeros((8, 128), F32), unroll=8)
+        x = out_p[...]
+        swapped = pltpu.roll(x, TSTEP, 1)
+        low = row_lane < TSTEP
+        return jnp.concatenate([jnp.where(low, x, swapped), jnp.where(low, swapped, x)], axis=0)
+
+    forward = sweep(mm, False)
+
+    cc[...] = rhs_s[...] - coupled(0, lower, pltpu.roll(forward, 1, 0))
+    trace_of_solution(cc, 0, filled)
+
+    backward = sweep(nn, True)
+
+    cc[...] = cc[...] - coupled(1, upper, pltpu.roll(backward, SLOTS - 1, 0))
 
     send_lane = lanes(SLOTS, WIDE)
     ret[...] = jnp.zeros((SLOTS, WIDE), F32)
 
     def solve(i, carry):
         total, given = ret[...], cc[...]
-        for b in range(18):
-            b = i * 18 + b
+        for b in range(54):
+            b = i * 54 + b
             total = jnp.where(send_lane == b, lane_sums(slab[b] * given), total)
         ret[...] = total
         return carry
 
-    lax.fori_loop(0, BLOCK // 18, solve, 0)
+    lax.fori_loop(0, BLOCK // 54, solve, 0)
     both = jnp.concatenate([ret[...], rhs_s[...]], axis=1)
-    answer = dot(to_slot, both, precision=HIGHEST)
+    answer = pick_rows(to_slot, both)
     send[:, 0, :] = jnp.concatenate([answer[:, 0:128], answer[:, 256:384], jnp.where(slot_lane < TSTEP, answer[:, 128:256], pltpu.roll(answer[:, 384:512], TSTEP, 1))], axis=1)
     exchange(send, back, 3)
     finish(send, back, 3)
-    answer = dot(jnp.transpose(pick_owner), back[:, 0, :], precision=HIGHEST)
+    answer = pick_rows(jnp.transpose(pick_owner), back[:, 0, :])
     third = answer[:, 256:384]
     fixed = jnp.concatenate([answer[:, 0:128], third], axis=1)
     kept = jnp.concatenate([answer[:, 128:256], pltpu.roll(third, TSTEP, 1)], axis=1)
-    ns_out[...] = fixed[0:ELEM, 0:BLOCK]
-    res_out[...] = rs_ref[...] - kept[0:ELEM, 0:BLOCK]
+    out[0] = fixed[0:ELEM, 0:BLOCK]
+    out[1] = rs_ref[...] - kept[0:ELEM, 0:BLOCK]
 
 
 def local(groups, owners, flow_state, right_side, diag_block, face_scale, face_pattern, neighbour, templates, line_inverse, line_scale, line_pattern, elem_line):
@@ -466,11 +474,11 @@
     vmem = pl.BlockSpec(memory_space=pltpu.VMEM)
     anywhere = pl.BlockSpec(memory_space=pl.ANY)
     message = pltpu.VMEM((owners, 1, MSG), F32)
-    correction, removed = pl.pallas_call(
+    both = pl.pallas_call(
         functools.partial(kernel, groups, owners),
-        out_shape=(jax.ShapeDtypeStruct((ELEM, BLOCK), F32), jax.ShapeDtypeStruct((ELEM, BLOCK), F32)),
+        out_shape=jax.ShapeDtypeStruct((2, ELEM, BLOCK), F32),
         in_specs=[anywhere] * 11,
-        out_specs=(vmem, vmem),
+        out_specs=vmem,
         scratch_shapes=[
             pltpu.VMEM((ELEM, BLOCK), F32),
             pltpu.VMEM((ELEM, BLOCK), F32),
@@ -488,20 +496,20 @@
             pltpu.VMEM((3, EROWS, WIDE), BF16),
             pltpu.VMEM((TALL, WIDE), F32),
             pltpu.VMEM((TALL, WIDE), BF16),
-            pltpu.VMEM((WIDE, TALL), BF16),
+            pltpu.VMEM((2 * TALL, WIDE), BF16),
+            pltpu.VMEM((2 * WIDE, TALL), BF16),
             pltpu.VMEM((4, EROWS, WIDE), F32),
             pltpu.VMEM((2, SLOTS, WIDE), F32),
             pltpu.VMEM((4, WIDE, TALL), BF16),
             pltpu.VMEM((WIDE, 128), BF16),
             pltpu.VMEM((BLOCK, SLOTS, WIDE), F32),
-            pltpu.VMEM((SLOTS * MROWS, 128), F32),
-            pltpu.VMEM((SLOTS * MROWS, 128), F32),
-            pltpu.VMEM((TRACE, SLOTS, 128), F32),
+            pltpu.VMEM((SLOTS * TSTEP, 128), F32),
+            pltpu.VMEM((SLOTS * TSTEP, 128), F32),
             pltpu.VMEM((EROWS, WIDE), F32),
-            pltpu.VMEM((SLOTS, 128), F32),
-            pltpu.VMEM((SLOTS, 128), F32),
-            pltpu.VMEM((SLOTS, 128), F32),
-            pltpu.VMEM((SLOTS, 128), F32),
+            pltpu.VMEM((SLOTS * TSTEP, 128), F32),
+            pltpu.VMEM((LEN, 8, 128), F32),
+            pltpu.VMEM((LEN, 8, 128), F32),
+            pltpu.VMEM((LEN, 128), F32),
             pltpu.VMEM((SLOTS, WIDE), F32),
             pltpu.VMEM((SLOTS, WIDE), F32),
             message,
@@ -514,7 +522,7 @@
         ],
         compiler_params=pltpu.CompilerParams(collective_id=0, has_side_effects=True, vmem_limit_bytes=56 * 1024 * 1024),
     )(*operands)
-    return flow_state + correction, right_side - removed
+    return flow_state + both[0], right_side - both[1]
 
 
 def solution(mesh):

time: 60.7 us -> 54.3 us (0.89)
  Pallas kernels: 56.9 us -> 51.9 us
  other arithmetic: 2.76 us -> 1.41 us
    pallas_call x1, Pallas kernels: 56.9 us -> 51.9 us  [local(): pl.pallas_call(functools.partial(kernel, groups, owners), out_shape=jax.S...]
    add x1 -> x0, other arithmetic: 1.38 us -> none  [local(): return (flow_state + correction, right_side - removed)]
where the time goes in v3:
time: 54.3 us; the launch traced here: 54 us
  Pallas kernels  51.9 us (96%)
  other arithmetic  1.41 us (3%)
  between operations  0.67 us (1%)
    pallas_call x1, Pallas kernels, local(): pl.pallas_call(functools.partial(kernel, groups, owners), out_shape=jax.S...  51.9 us
    sub x1, other arithmetic, local(): return (flow_state + both[0], right_side - both[1])  1.41 us

profile of v3, /device:TPU:1, one launch (start us, length us, event | category | flops | bytes accessed | tf_op | source)
XLA Modules:
  0.0 54.0 jit_solution(6524341427947332105)
XLA Ops:
  0.6 0.0 copy-start
  0.6 0.0 copy-start.1
  0.7 51.9 %shard_map.122 = f32[2,26,162]{2,1,0:T(8,128)} custom-call(f32[26,162]{1,0:T(8,128)} %fs_hbm.1, f32[26,162]{1,0:T(8,128)} %rs_hbm.1, bf16[26,26244]{1,0:T(8,128)(2,1)} %diag_hbm.1, bf16[26,4,162]{2,1,0:T(4,128)(2,1)} %fsc_hbm.1, s32[4,26]{1,0:T(4,128)} %bitcast.10, s32[4,26]{1,0:T(4,128)} %bitcast.11, bf16[6,54,162]{2,1,0:T(8,128)(2,1)} %bitcast.9, ...), custom_call_target="tpu_custom_call" | custom-call | tf_op jit(solution)/shard_map/pallas_call | solution.py:477
  52.6 0.0 copy-done
  52.6 0.0 copy-done.1
  52.6 1.4 %bitcast_subtract_fusion = (f32[26,162]{1,0:T(8,128)}, f32[26,162]{1,0:T(8,128)}) fusion(f32[26,162]{1,0:T(8,128)S(1)} %copy-done, f32[2,26,162]{2,1,0:T(8,128)} %shard_map.122, f32[26,162]{1,0:T(8,128)S(1)} %copy-done.1), kind=kLoop, calls=%fused_computation | loop fusion | flops 8424 | bytes 101088 | tf_op jit(solution)/shard_map/sub | solution.py:525
Async XLA Ops:
  0.6 52.0 %copy-start = (f32[26,162]{1,0:T(8,128)S(1)}, f32[26,162]{1,0:T(8,128)}, u32[]{:S(2)}) copy-start(f32[26,162]{1,0:T(8,128)} %rs_hbm.1) | copy-start | bytes 50548
  0.6 52.0 %copy-start.1 = (f32[26,162]{1,0:T(8,128)S(1)}, f32[26,162]{1,0:T(8,128)}, u32[]{:S(2)}) copy-start(f32[26,162]{1,0:T(8,128)} %fs_hbm.1) | copy-start | bytes 50548

commit v4 on v3

--- a/solution.py
+++ b/solution.py
@@ -24,7 +24,6 @@
 TSTEP = 64
 TALL = NPAT * TSTEP
 MROWS = 56
-MSG = 384
 
 
 def trace_column(face_id, width):
@@ -123,9 +122,14 @@
     out_p,
     cc,
     rhs_s,
-    send,
-    recv,
-    back,
+    send_t,
+    recv_t,
+    send_p,
+    recv_p,
+    send_r,
+    back_r,
+    send_c,
+    back_c,
     ret,
     dsem,
     ssem,
@@ -228,7 +232,76 @@
             slab[i * 23 + b] = block_row(linv, SLOTS, (i * 23 + b) * BLOCK)
         return carry
 
-    lax.fori_loop(0, 4, rows_of, 0)
+    lax.fori_loop(0, (BLOCK - 1) // 23, rows_of, 0)
+    tail = linv[:, (BLOCK - 1) * BLOCK - 98 : BLOCK * BLOCK].astype(F32)
+    slab[BLOCK - 1] = jnp.zeros((SLOTS, WIDE), F32)
+    slab[BLOCK - 1, :, 0:BLOCK] = tail[:, 98 : 98 + BLOCK]
+
+    slot = columns[0:EROWS, 8:9]
+    local_slot = slot - jnp.floor(slot * (1.0 / SLOTS)) * SLOTS
+    traces = dot(rounded, lpick[...])
+    traces = jnp.where(lanes(EROWS, 128) == 127, local_slot + 1.0, traces)
+    owner_row = jnp.floor(ints[8:9, 0:EROWS] * (1.0 / SLOTS))
+    pick_owner = jnp.where(lax.broadcasted_iota(jnp.int32, (owners, EROWS), 0).astype(F32) == owner_row, 1.0, 0.0)
+    send_t[:, 0, :] = dot(pick_owner.astype(BF16), traces.astype(BF16))
+
+    def send_one(source, target, index, other):
+        pltpu.make_async_remote_copy(
+            src_ref=source.at[other],
+            dst_ref=target.at[me],
+            send_sem=ssem.at[index],
+            recv_sem=rsem.at[index],
+            device_id=(reg, other),
+            device_id_type=MESH,
+        ).start()
+
+    def exchange(source, target, index):
+        def four(i, carry):
+            for other in others(i):
+                send_one(source, target, index, other)
+            return carry
+
+        lax.fori_loop(0, owners // 4 - 1, four, 0)
+        for other in others(owners // 4 - 1)[:3]:
+            send_one(source, target, index, other)
+        target[pl.ds(me, 1)] = source[pl.ds(me, 1)]
+
+    def finish(source, target, index):
+        whole = pltpu.make_async_remote_copy(
+            src_ref=source.at[pl.ds(0, owners - 1)],
+            dst_ref=target.at[pl.ds(0, owners - 1)],
+            send_sem=ssem.at[index],
+            recv_sem=rsem.at[index],
+            device_id=(reg, lax.rem(me + 1, owners)),
+            device_id_type=MESH,
+        )
+        whole.wait_send()
+        whole.wait_recv()
+
+    kinds = [columns[0:SLOTS, 9 + i : 10 + i] for i in range(2)]
+    chosen = [jnp.where((lanes(SLOTS, TALL) // TSTEP).astype(F32) == kind, 1.0, 0.0) for kind in kinds]
+    low_half = lanes(SLOTS, 128) < TSTEP
+    own_half = lanes(SLOTS, 128) // TSTEP == lax.broadcasted_iota(jnp.int32, (SLOTS, 128), 0) // LEN
+
+    def store_rows(target, m, x):
+        target[pl.ds(m, LEN, stride=2 * TSTEP), :] = x[0:LEN]
+        target[pl.ds(m + TSTEP, LEN, stride=2 * TSTEP), :] = x[LEN:]
+
+    def small_rows(i, carry):
+        parts = []
+        for u in range(9):
+            m = 9 * i + u
+            for x in (slab[3 * m + 2] * lsc[0], slab[3 * m] * lsc[1]):
+                parts.append(jnp.concatenate(halves(x), axis=1))
+        product = dot(jnp.concatenate(parts, axis=0), tpt[...])
+        for u in range(9):
+            for kind, target in enumerate((mm, nn)):
+                at = (u * 2 + kind) * SLOTS
+                x = product[at : at + SLOTS] * chosen[kind]
+                x = x[:, 0:128] + x[:, 128:256] + x[:, 256:384]
+                x = x + pltpu.roll(x, TSTEP, 1)
+                store_rows(target, 9 * i + u, jnp.where(own_half, x, 0.0))
+        return carry
 
     pl.semaphore_wait(bar, owners + 1)
     up = pltpu.make_async_remote_copy(
@@ -239,10 +312,8 @@
     )
     up.start()
     down.start()
-    lax.fori_loop(4, (BLOCK - 1) // 23, rows_of, 0)
-    tail = linv[:, (BLOCK - 1) * BLOCK - 98 : BLOCK * BLOCK].astype(F32)
-    slab[BLOCK - 1] = jnp.zeros((SLOTS, WIDE), F32)
-    slab[BLOCK - 1, :, 0:BLOCK] = tail[:, 98 : 98 + BLOCK]
+    exchange(send_t, recv_t, 2)
+    lax.fori_loop(0, 3, small_rows, 0)
     up.wait()
     down.wait()
 
@@ -267,79 +338,10 @@
         total = total + terms[side * EROWS : (side + 1) * EROWS] * fsc[side]
     xs[...] = jnp.zeros((EROWS, WIDE), F32)
     xs[0:ELEM, 0:BLOCK] = rs_ref[...]
-    partial = xs[...] - total
-
-    slot = columns[0:EROWS, 8:9]
-    owner = jnp.floor(slot * (1.0 / SLOTS))
-    local_slot = slot - owner * SLOTS
-    traces = dot(rounded, lpick[...])
-    traces = jnp.where(lanes(EROWS, 128) == 127, local_slot + 1.0, traces)
-    owner_row = jnp.floor(ints[8:9, 0:EROWS] * (1.0 / SLOTS))
-    pick_owner = jnp.where(lax.broadcasted_iota(jnp.int32, (owners, EROWS), 0).astype(F32) == owner_row, 1.0, 0.0)
-    payload = jnp.concatenate([traces, partial], axis=1)
-    send[:, 0, :] = pick_rows(pick_owner, payload)
-
-    def exchange(source, target, index):
-        def one(other):
-            pltpu.make_async_remote_copy(
-                src_ref=source.at[other],
-                dst_ref=target.at[me],
-                send_sem=ssem.at[index],
-                recv_sem=rsem.at[index],
-                device_id=(reg, other),
-                device_id_type=MESH,
-            ).start()
-
-        def four(i, carry):
-            for other in others(i):
-                one(other)
-            return carry
-
-        lax.fori_loop(0, owners // 4 - 1, four, 0)
-        for other in others(owners // 4 - 1)[:3]:
-            one(other)
-        target[pl.ds(me, 1)] = source[pl.ds(me, 1)]
-
-    def finish(source, target, index):
-        whole = pltpu.make_async_remote_copy(
-            src_ref=source.at[pl.ds(0, owners - 1)],
-            dst_ref=target.at[pl.ds(0, owners - 1)],
-            send_sem=ssem.at[index],
-            recv_sem=rsem.at[index],
-            device_id=(reg, lax.rem(me + 1, owners)),
-            device_id_type=MESH,
-        )
-        whole.wait_send()
-        whole.wait_recv()
-
-    exchange(send, recv, 2)
-
-    kinds = [columns[0:SLOTS, 9 + i : 10 + i] for i in range(2)]
-    chosen = [jnp.where((lanes(SLOTS, TALL) // TSTEP).astype(F32) == kind, 1.0, 0.0) for kind in kinds]
-    low_half = lanes(SLOTS, 128) < TSTEP
-    own_half = lanes(SLOTS, 128) // TSTEP == lax.broadcasted_iota(jnp.int32, (SLOTS, 128), 0) // LEN
-
-    def store_rows(target, m, x):
-        target[pl.ds(m, LEN, stride=2 * TSTEP), :] = x[0:LEN]
-        target[pl.ds(m + TSTEP, LEN, stride=2 * TSTEP), :] = x[LEN:]
-
-    def small_rows(i, carry):
-        parts = []
-        for u in range(9):
-            m = 9 * i + u
-            for x in (slab[3 * m + 2] * lsc[0], slab[3 * m] * lsc[1]):
-                parts.append(jnp.concatenate(halves(x), axis=1))
-        product = dot(jnp.concatenate(parts, axis=0), tpt[...])
-        for u in range(9):
-            for kind, target in enumerate((mm, nn)):
-                at = (u * 2 + kind) * SLOTS
-                x = product[at : at + SLOTS] * chosen[kind]
-                x = x[:, 0:128] + x[:, 128:256] + x[:, 256:384]
-                x = x + pltpu.roll(x, TSTEP, 1)
-                store_rows(target, 9 * i + u, jnp.where(own_half, x, 0.0))
-        return carry
-
-    lax.fori_loop(0, TRACE // 9, small_rows, 0)
+    send_p[:, 0, :] = pick_rows(pick_owner, xs[...] - total)
+    exchange(send_p, recv_p, 3)
+
+    lax.fori_loop(3, TRACE // 9, small_rows, 0)
     for m in range(TRACE, TSTEP):
         for target in (mm, nn, gcol):
             store_rows(target, m, jnp.zeros((SLOTS, 128), F32))
@@ -354,12 +356,11 @@
 
     lax.fori_loop(0, LEN // 2, turn, 0, unroll=8)
 
-    finish(send, recv, 2)
-    got = recv[:, 0, :]
-    slot_column = got[:, 127:128] - 1.0
-    to_slot = jnp.where(lanes(owners, SLOTS).astype(F32) == slot_column, 1.0, 0.0)
+    finish(send_t, recv_t, 2)
+    got = recv_t[:, 0, :]
+    to_slot = jnp.where(lanes(owners, SLOTS).astype(F32) == got[:, 127:128] - 1.0, 1.0, 0.0)
     from_source = jnp.transpose(to_slot)
-    gathered = pick_rows(from_source, got)
+    line_traces = dot(from_source.astype(BF16), got.astype(BF16))
     filled = jnp.sum(from_source, axis=1, keepdims=True)
     place = lax.rem(lax.broadcasted_iota(jnp.int32, (SLOTS, 1), 0), LEN)
     lower = jnp.where(place > 0, filled, 0.0)
@@ -370,15 +371,16 @@
         spread = jnp.concatenate([x, x, x], axis=1) * chosen[kind]
         return dot(jnp.concatenate(halves(spread), axis=1), tp2[...]) * lsc[kind]
 
-    line_traces = gathered[:, 0:128]
     swapped = pltpu.roll(line_traces, TSTEP, 1)
     tops = jnp.where(low_half, line_traces, swapped)
     bottoms = jnp.where(low_half, swapped, line_traces)
-    rhs = gathered[:, 128:384] - coupled(0, lower, pltpu.roll(tops, 1, 0)) - coupled(1, upper, pltpu.roll(bottoms, SLOTS - 1, 0))
-    rhs_s[...] = rhs
-
-    slot_lane = lanes(SLOTS, 128)
+    terms = coupled(0, lower, pltpu.roll(tops, 1, 0)) + coupled(1, upper, pltpu.roll(bottoms, SLOTS - 1, 0))
     row_lane = lanes(LEN, 128)
+    gates = jnp.where(row_lane < TSTEP, filled[0:LEN], filled[LEN:])
+    gate_p[...] = jnp.broadcast_to(gates[:, None, :], (LEN, 8, 128))
+    finish(send_p, recv_p, 3)
+    rhs_s[...] = pick_rows(from_source, recv_p[:, 0, :]) - terms
+
 
     def trace_of_solution(given, first, gate):
         x, rows = given[...], jnp.zeros((LEN, 128), F32)
@@ -390,17 +392,18 @@
             rows = jnp.where(row_lane == m, value[0:LEN], jnp.where(row_lane == m + TSTEP, value[LEN:], rows))
         rows_p[...] = jnp.broadcast_to(rows[:, None, :], (LEN, 8, 128))
 
-    gates = jnp.where(row_lane < TSTEP, filled[0:LEN], filled[LEN:])
-    gate_p[...] = jnp.broadcast_to(gates[:, None, :], (LEN, 8, 128))
     trace_of_solution(rhs_s, 2, None)
+
+    send_r[:, 0, :] = pick_rows(to_slot, rhs_s[...])
 
     tiles = MROWS // 8
     place8 = [lax.broadcasted_iota(jnp.int32, (tiles, 8, 128), i) for i in range(3)]
     eye = jnp.where(place8[2] % TSTEP == 8 * place8[0] + place8[1], 1.0, 0.0)
     first_line = place8[2] < TSTEP
 
-    def sweep(matrices, reverse):
-        def pair(i, row):
+    def sweep(matrices, reverse, beside):
+        def pair(i, row, last=False):
+            beside(i, last)
             first = LEN - 1 - 2 * i if reverse else 2 * i
             second = first - 1 if reverse else first + 1
             at = pl.multiple_of(first * 2 * TSTEP, 128)
@@ -417,18 +420,24 @@
             out_p[pl.ds(second, 1), :] = row[0:1]
             return row
 
-        lax.fori_loop(0, LEN // 2, pair, jnp.zeros((8, 128), F32), unroll=8)
+        pair(LEN // 2 - 1, lax.fori_loop(0, LEN // 2 - 1, pair, jnp.zeros((8, 128), F32), unroll=5), True)
         x = out_p[...]
         swapped = pltpu.roll(x, TSTEP, 1)
         low = row_lane < TSTEP
         return jnp.concatenate([jnp.where(low, x, swapped), jnp.where(low, swapped, x)], axis=0)
 
-    forward = sweep(mm, False)
+    def send_four(i, last):
+        for other in others(i)[: 3 if last else 4]:
+            send_one(send_r, back_r, 4, other)
+
+    assert owners == 2 * LEN
+    forward = sweep(mm, False, send_four)
+    back_r[pl.ds(me, 1)] = send_r[pl.ds(me, 1)]
 
     cc[...] = rhs_s[...] - coupled(0, lower, pltpu.roll(forward, 1, 0))
     trace_of_solution(cc, 0, filled)
 
-    backward = sweep(nn, True)
+    backward = sweep(nn, True, lambda i, last: None)
 
     cc[...] = cc[...] - coupled(1, upper, pltpu.roll(backward, SLOTS - 1, 0))
 
@@ -444,17 +453,13 @@
         return carry
 
     lax.fori_loop(0, BLOCK // 54, solve, 0)
-    both = jnp.concatenate([ret[...], rhs_s[...]], axis=1)
-    answer = pick_rows(to_slot, both)
-    send[:, 0, :] = jnp.concatenate([answer[:, 0:128], answer[:, 256:384], jnp.where(slot_lane < TSTEP, answer[:, 128:256], pltpu.roll(answer[:, 384:512], TSTEP, 1))], axis=1)
-    exchange(send, back, 3)
-    finish(send, back, 3)
-    answer = pick_rows(jnp.transpose(pick_owner), back[:, 0, :])
-    third = answer[:, 256:384]
-    fixed = jnp.concatenate([answer[:, 0:128], third], axis=1)
-    kept = jnp.concatenate([answer[:, 128:256], pltpu.roll(third, TSTEP, 1)], axis=1)
-    out[0] = fixed[0:ELEM, 0:BLOCK]
-    out[1] = rs_ref[...] - kept[0:ELEM, 0:BLOCK]
+    send_c[:, 0, :] = pick_rows(to_slot, ret[...])
+    exchange(send_c, back_c, 5)
+    pick_element = jnp.transpose(pick_owner)
+    finish(send_r, back_r, 4)
+    out[1] = rs_ref[...] - pick_rows(pick_element, back_r[:, 0, :])[0:ELEM, 0:BLOCK]
+    finish(send_c, back_c, 5)
+    out[0] = pick_rows(pick_element, back_c[:, 0, :])[0:ELEM, 0:BLOCK]
 
 
 def local(groups, owners, flow_state, right_side, diag_block, face_scale, face_pattern, neighbour, templates, line_inverse, line_scale, line_pattern, elem_line):
@@ -473,7 +478,6 @@
     )
     vmem = pl.BlockSpec(memory_space=pltpu.VMEM)
     anywhere = pl.BlockSpec(memory_space=pl.ANY)
-    message = pltpu.VMEM((owners, 1, MSG), F32)
     both = pl.pallas_call(
         functools.partial(kernel, groups, owners),
         out_shape=jax.ShapeDtypeStruct((2, ELEM, BLOCK), F32),
@@ -512,13 +516,11 @@
             pltpu.VMEM((LEN, 128), F32),
             pltpu.VMEM((SLOTS, WIDE), F32),
             pltpu.VMEM((SLOTS, WIDE), F32),
-            message,
-            message,
-            message,
+            *[pltpu.VMEM((owners, 1, width), F32) for width in (128, 128) + (WIDE,) * 6],
             pltpu.VMEM((SLOTS, WIDE), F32),
             pltpu.SemaphoreType.DMA((2 + 9,)),
-            pltpu.SemaphoreType.DMA((4,)),
-            pltpu.SemaphoreType.DMA((4,)),
+            pltpu.SemaphoreType.DMA((6,)),
+            pltpu.SemaphoreType.DMA((6,)),
         ],
         compiler_params=pltpu.CompilerParams(collective_id=0, has_side_effects=True, vmem_limit_bytes=56 * 1024 * 1024),
     )(*operands)

time: 54.3 us -> 52.7 us (0.971)
  Pallas kernels: 51.9 us -> 50.3 us
    pallas_call x1, Pallas kernels: 51.9 us -> 50.3 us  [local(): pl.pallas_call(functools.partial(kernel, groups, owners), out_shape=jax.S...]
where the time goes in v4:
time: 52.7 us; the launch traced here: 52.4 us
  Pallas kernels  50.3 us (95%)
  other arithmetic  1.41 us (3%)
  between operations  0.67 us (1%)
    pallas_call x1, Pallas kernels, local(): pl.pallas_call(functools.partial(kernel, groups, owners), out_shape=jax.S...  50.3 us
    sub x1, other arithmetic, local(): return (flow_state + both[0], right_side - both[1])  1.41 us

profile of v4, /device:TPU:1, one launch (start us, length us, event | category | flops | bytes accessed | tf_op | source)
XLA Modules:
  0.0 52.4 jit_solution(4132098944323551245)
XLA Ops:
  0.6 0.0 copy-start
  0.6 0.0 copy-start.1
  0.7 50.3 %shard_map.122 = f32[2,26,162]{2,1,0:T(8,128)} custom-call(f32[26,162]{1,0:T(8,128)} %fs_hbm.1, f32[26,162]{1,0:T(8,128)} %rs_hbm.1, bf16[26,26244]{1,0:T(8,128)(2,1)} %diag_hbm.1, bf16[26,4,162]{2,1,0:T(4,128)(2,1)} %fsc_hbm.1, s32[4,26]{1,0:T(4,128)} %bitcast.10, s32[4,26]{1,0:T(4,128)} %bitcast.11, bf16[6,54,162]{2,1,0:T(8,128)(2,1)} %bitcast.9, ...), custom_call_target="tpu_custom_call" | custom-call | tf_op jit(solution)/shard_map/pallas_call | solution.py:481
  51.0 0.0 copy-done
  51.0 0.0 copy-done.1
  51.0 1.4 %bitcast_subtract_fusion = (f32[26,162]{1,0:T(8,128)}, f32[26,162]{1,0:T(8,128)}) fusion(f32[26,162]{1,0:T(8,128)S(1)} %copy-done, f32[2,26,162]{2,1,0:T(8,128)} %shard_map.122, f32[26,162]{1,0:T(8,128)S(1)} %copy-done.1), kind=kLoop, calls=%fused_computation | loop fusion | flops 8424 | bytes 101088 | tf_op jit(solution)/shard_map/sub | solution.py:527
Async XLA Ops:
  0.6 50.3 %copy-start = (f32[26,162]{1,0:T(8,128)S(1)}, f32[26,162]{1,0:T(8,128)}, u32[]{:S(2)}) copy-start(f32[26,162]{1,0:T(8,128)} %rs_hbm.1) | copy-start | bytes 50548
  0.6 50.3 %copy-start.1 = (f32[26,162]{1,0:T(8,128)S(1)}, f32[26,162]{1,0:T(8,128)}, u32[]{:S(2)}) copy-start(f32[26,162]{1,0:T(8,128)} %fs_hbm.1) | copy-start | bytes 50548

commit v5 on v4

--- a/solution.py
+++ b/solution.py
@@ -401,7 +401,7 @@
     eye = jnp.where(place8[2] % TSTEP == 8 * place8[0] + place8[1], 1.0, 0.0)
     first_line = place8[2] < TSTEP
 
-    def sweep(matrices, reverse, beside):
+    def steps(matrices, reverse, beside):
         def pair(i, row, last=False):
             beside(i, last)
             first = LEN - 1 - 2 * i if reverse else 2 * i
@@ -420,39 +420,65 @@
             out_p[pl.ds(second, 1), :] = row[0:1]
             return row
 
-        pair(LEN // 2 - 1, lax.fori_loop(0, LEN // 2 - 1, pair, jnp.zeros((8, 128), F32), unroll=5), True)
-        x = out_p[...]
+        return pair
+
+    def both_halves(x):
         swapped = pltpu.roll(x, TSTEP, 1)
-        low = row_lane < TSTEP
+        low = lanes(x.shape[0], 128) < TSTEP
         return jnp.concatenate([jnp.where(low, x, swapped), jnp.where(low, swapped, x)], axis=0)
+
+    nothing = jnp.zeros((8, 128), F32)
 
     def send_four(i, last):
         for other in others(i)[: 3 if last else 4]:
             send_one(send_r, back_r, 4, other)
 
     assert owners == 2 * LEN
-    forward = sweep(mm, False, send_four)
+    pair = steps(mm, False, send_four)
+    pair(LEN // 2 - 1, lax.fori_loop(0, LEN // 2 - 1, pair, nothing, unroll=5), True)
+    forward = both_halves(out_p[...])
     back_r[pl.ds(me, 1)] = send_r[pl.ds(me, 1)]
 
     cc[...] = rhs_s[...] - coupled(0, lower, pltpu.roll(forward, 1, 0))
     trace_of_solution(cc, 0, filled)
 
-    backward = sweep(nn, True, lambda i, last: None)
-
-    cc[...] = cc[...] - coupled(1, upper, pltpu.roll(backward, SLOTS - 1, 0))
-
-    send_lane = lanes(SLOTS, WIDE)
-    ret[...] = jnp.zeros((SLOTS, WIDE), F32)
-
-    def solve(i, carry):
-        total, given = ret[...], cc[...]
-        for b in range(54):
-            b = i * 54 + b
-            total = jnp.where(send_lane == b, lane_sums(slab[b] * given), total)
-        ret[...] = total
-        return carry
-
-    lax.fori_loop(0, BLOCK // 54, solve, 0)
+    half = LEN // 2
+
+    def part(x, high):
+        start = half if high else 0
+        return jnp.concatenate([x[start : start + half], x[start + LEN : start + LEN + half]], axis=0)
+
+    def finished(high, after):
+        x = jnp.where(part(upper, high) > 0.5, after, 0.0)
+        spread = jnp.concatenate([x, x, x], axis=1) * part(chosen[1], high)
+        term = dot(jnp.concatenate(halves(spread), axis=1), tp2[...]) * part(lsc[1], high)
+        return part(cc[...], high) - term
+
+    half_lane = lanes(LEN, WIDE)
+
+    def solve(b, given, high, total):
+        start = half if high else 0
+        rows = jnp.concatenate([slab[b, start : start + half], slab[b, start + LEN : start + LEN + half]], axis=0)
+        return jnp.where(half_lane == b, lane_sums(rows * given), total)
+
+    pair = steps(nn, True, lambda i, last: None)
+    row = lax.fori_loop(0, half // 2, pair, nothing, unroll=4)
+    given = finished(True, pltpu.roll(both_halves(out_p[half:LEN]), LEN - 1, 0))
+    total = jnp.zeros((LEN, WIDE), F32)
+    for i in range(half // 2):
+        row = pair(half // 2 + i, row)
+        for b in range(BLOCK * i // (half // 2), BLOCK * (i + 1) // (half // 2)):
+            total = solve(b, given, True, total)
+    ret[half:LEN] = total[0:half]
+    ret[half + LEN : 2 * LEN] = total[half:]
+
+    given = finished(False, both_halves(out_p[1 : half + 1]))
+    total = jnp.zeros((LEN, WIDE), F32)
+    for b in range(BLOCK):
+        total = solve(b, given, False, total)
+    ret[0:half] = total[0:half]
+    ret[LEN : LEN + half] = total[half:]
+
     send_c[:, 0, :] = pick_rows(to_slot, ret[...])
     exchange(send_c, back_c, 5)
     pick_element = jnp.transpose(pick_owner)

time: 52.7 us -> 51.9 us (0.985)
  Pallas kernels: 50.3 us -> 49.5 us
    pallas_call x1, Pallas kernels: 50.3 us -> 49.5 us  [local(): pl.pallas_call(functools.partial(kernel, groups, owners), out_shape=jax.S...]
where the time goes in v5:
time: 51.9 us; the launch traced here: 51.6 us
  Pallas kernels  49.5 us (95%)
  other arithmetic  1.41 us (3%)
  between operations  0.67 us (1%)
    pallas_call x1, Pallas kernels, local(): pl.pallas_call(functools.partial(kernel, groups, owners), out_shape=jax.S...  49.5 us
    sub x1, other arithmetic, local(): return (flow_state + both[0], right_side - both[1])  1.41 us

profile of v5, /device:TPU:1, one launch (start us, length us, event | category | flops | bytes accessed | tf_op | source)
XLA Modules:
  0.0 51.6 jit_solution(3201253122042753139)
XLA Ops:
  0.6 0.0 copy-start
  0.6 0.0 copy-start.1
  0.7 49.5 %shard_map.122 = f32[2,26,162]{2,1,0:T(8,128)} custom-call(f32[26,162]{1,0:T(8,128)} %fs_hbm.1, f32[26,162]{1,0:T(8,128)} %rs_hbm.1, bf16[26,26244]{1,0:T(8,128)(2,1)} %diag_hbm.1, bf16[26,4,162]{2,1,0:T(4,128)(2,1)} %fsc_hbm.1, s32[4,26]{1,0:T(4,128)} %bitcast.10, s32[4,26]{1,0:T(4,128)} %bitcast.11, bf16[6,54,162]{2,1,0:T(8,128)(2,1)} %bitcast.9, ...), custom_call_target="tpu_custom_call" | custom-call | tf_op jit(solution)/shard_map/pallas_call | solution.py:507
  50.2 0.0 copy-done
  50.2 0.0 copy-done.1
  50.2 1.4 %bitcast_subtract_fusion = (f32[26,162]{1,0:T(8,128)}, f32[26,162]{1,0:T(8,128)}) fusion(f32[26,162]{1,0:T(8,128)S(1)} %copy-done, f32[2,26,162]{2,1,0:T(8,128)} %shard_map.122, f32[26,162]{1,0:T(8,128)S(1)} %copy-done.1), kind=kLoop, calls=%fused_computation | loop fusion | flops 8424 | bytes 101088 | tf_op jit(solution)/shard_map/sub | solution.py:553
Async XLA Ops:
  0.6 49.5 %copy-start = (f32[26,162]{1,0:T(8,128)S(1)}, f32[26,162]{1,0:T(8,128)}, u32[]{:S(2)}) copy-start(f32[26,162]{1,0:T(8,128)} %rs_hbm.1) | copy-start | bytes 50548
  0.6 49.5 %copy-start.1 = (f32[26,162]{1,0:T(8,128)S(1)}, f32[26,162]{1,0:T(8,128)}, u32[]{:S(2)}) copy-start(f32[26,162]{1,0:T(8,128)} %fs_hbm.1) | copy-start | bytes 50548
